TPU v7x, 1024 devices: a whole 4x4x32 slice. The times are simulated.
1024 devices in a mesh: dp: 32 (over z_lo, y), seq: 32 (over x, z_hi, core).
Axes of the slice: x: 4, y: 4, z: 32 (z_hi: 4, z_lo: 8; z = z_hi * 8 + z_lo), core: 2. Of those that a mesh axis runs over, the one named last changes fastest.
Arguments:
- attention_out: bfloat16 [131072, 1152], P(('dp', 'seq')), may hold values from -24 to 24
- upstream: bfloat16 [131072, 1152], P(('dp', 'seq')), may hold values from -6 to 6
- tap_slots: bfloat16 [3, 65536, 4608], P(None, ('dp', 'seq')), may hold values from -6 to 6
- owner_map: int32 [32768, 1], P(('dp', 'seq')), may hold values from 0 to 31; in each aligned block of 32 rows (0 to 31, 32 to 63, ...) at most 2 rows name the same one
- out_proj: bfloat16 [1152, 1152], replicated, may hold values from -0.1875 to 0.1875
Outputs:
- stream_grad: bfloat16 [131072, 1152], P(('dp', 'seq'))
- attention_grad: bfloat16 [131072, 1152], P(('dp', 'seq'))
- shallow_grads: bfloat16 [2, 131072, 1152], P(None, ('dp', 'seq'))
- proj_grad: float32 [1152, 1152], P('dp', 'seq')
Inputs may be any that keep to these rules, and one draw needn't show every extreme that they name: `owner_map`: within the 32 merged tokens of one device no owner is named more than 2 times, a bound that some block reaches.
All inputs are finite; a program needn't handle non-finite values.
Results may differ from a plain program's by a relative error of at most 0.0051.
Values may be sent and summed in bfloat16 or wider, within the bound.
No kernel may reach another device: no remote copies, remote signals or barrier semaphores. Data moves between devices by JAX's collectives and lax.ppermute only.
A program may use at most 64 MiB of HBM per device.

v0:
```python
import math

import jax
import jax.numpy as jnp
from jax import lax
from jax.sharding import PartitionSpec as P

LEVELS = 3


def on_device(attention_out, upstream, tap_slots, owner_map, out_proj):
    owners = owner_map[:, 0]
    seq_count = lax.axis_size("seq")
    dp_count = lax.axis_size("dp")
    capacity = tap_slots.shape[1] // seq_count
    onehot = (owners[:, None] == jnp.arange(seq_count, dtype=jnp.int32)[None, :]).astype(jnp.int32)
    before = jnp.cumsum(onehot, axis=0) - onehot
    rank = jnp.sum(before * onehot, axis=1)
    slot_index = owners * capacity + rank
    patches = attention_out.shape[0]
    width = attention_out.shape[1]
    received = lax.all_to_all(tap_slots, "seq", split_axis=1, concat_axis=1, tiled=True)
    taps = jnp.take(received, slot_index, axis=1).reshape(received.shape[0], patches, width)
    deepest = taps[LEVELS - 1]
    stream = (upstream.astype(jnp.float32) + deepest.astype(jnp.float32)).astype(jnp.bfloat16)
    attention_grad = lax.dot_general(
        stream, out_proj, (((1,), (1,)), ((), ())), preferred_element_type=jnp.float32
    ).astype(jnp.bfloat16)
    factor = jnp.float32(1.0 / math.sqrt(patches * dp_count * seq_count))
    own_rows = lax.psum_scatter(
        lax.dot_general(
            attention_out, stream, (((0,), (0,)), ((), ())), preferred_element_type=jnp.float32
        ),
        "dp",
        scatter_dimension=0,
        tiled=True,
    )
    proj_grad = lax.psum_scatter(own_rows, "seq", scatter_dimension=1, tiled=True) * factor
    shallow = taps[0 : LEVELS - 1]
    return (stream, attention_grad, shallow, proj_grad)


def solution(mesh):
    in_specs = (
        P(("dp", "seq"), None),
        P(("dp", "seq"), None),
        P(None, ("dp", "seq"), None),
        P(("dp", "seq"), None),
        P(),
    )
    out_specs = (
        P(("dp", "seq"), None),
        P(("dp", "seq"), None),
        P(None, ("dp", "seq"), None),
        P("dp", "seq"),
    )
    return jax.shard_map(
        on_device, mesh=mesh, in_specs=in_specs, out_specs=out_specs, check_vma=False
    )
```

profile of v0, /device:TPU:2, one launch (start us, length us, event | category | flops | bytes accessed | tf_op | source)
XLA Modules:
  0.0 972.6 jit_solution(7169112130157882801)
XLA Ops:
  7.2 4.6 copy.15
  11.7 31.7 %all-to-all-start = ((bf16[3,64,4608]{2,0,1:T(4,128)(2,1)}), bf16[3,64,4608]{2,0,1:T(4,128)(2,1)}, u32[]{:S(2)}, u32[]{:S(2)}) async-start(bf16[3,64,4608]{2,0,1:T(4,128)(2,1)} %copy.15), calls=%async_computation | async-start | bytes 4718592 | tf_op jit(solution)/shard_map/all_to_all | solution.py:22
  43.5 0.1 fusion.2
  43.6 0.2 select_reduce_fusion
  43.8 210.8 %all-to-all-done = bf16[3,64,4608]{2,0,1:T(4,128)(2,1)} async-done(((bf16[3,64,4608]{2,0,1:T(4,128)(2,1)}), bf16[3,64,4608]{2,0,1:T(4,128)(2,1)}, u32[]{:S(2)}, u32[]{:S(2)}) %all-to-all-start) | async-done | bytes 1769504 | tf_op jit(solution)/shard_map/all_to_all | solution.py:22
  254.6 4.2 gather_fusion
  258.8 1.9 select_bitcast_fusion
  260.7 1.0 copy-done.1
  261.7 2.6 fusion.1
  264.3 1.2 reshape.20
  265.5 1.0 add_convert_fusion
  266.5 4.3 convolution_bitcast_fusion
  270.9 1.3 dynamic-slice
  272.8 488.0 %all-reduce.5.cloned.1.call-done = f32[1152,1152]{0,1:T(8,128)} async-done(((f32[1152,1152]{0,1:T(8,128)}), f32[1152,1152]{0,1:T(8,128)}) %all-reduce.5.cloned.1.call-update) | async-done | bytes 5308432
  760.8 1.5 constant_dynamic-slice_fusion
  762.3 130.4 %fusion = f32[36,48]{0,1:T(8,128)} fusion(f32[36,1152]{0,1:T(8,128)S(1)} %constant_dynamic-slice_fusion), kind=kCustom, calls=%all-reduce-scatter | all-reduce-scatter fusion | flops 55297 | bytes 176896
  892.7 2.0 collective-permute-start.6
  894.8 3.3 collective-permute-start.5
  898.1 1.3 slice.17
  899.4 6.5 collective-permute-start.7
  905.9 1.3 dynamic-slice.6
  907.8 5.8 collective-permute-start.4
  913.6 20.0 %collective-permute-start.3 = (f32[36,48]{0,1:T(8,128)}, f32[36,48]{0,1:T(8,128)}, u32[]{:S(2)}, u32[]{:S(2)}) collective-permute-start(f32[36,48]{0,1:T(8,128)} %fusion), channel_id=1, source_target_pairs={{0,4},{1,5},{2,6},{3,7},{4,8},{5,9},{6,10},{7,11},{8,12},{9,13},{1... | collective-permute-start | bytes 20744
  933.6 1.9 collective-permute-start.2
  935.6 3.4 collective-permute-start.1
  939.0 11.6 %collective-permute-start = (f32[36,48]{0,1:T(8,128)}, f32[36,48]{0,1:T(8,128)}, u32[]{:S(2)}, u32[]{:S(2)}) collective-permute-start(f32[36,48]{0,1:T(8,128)} %fusion), channel_id=1, source_target_pairs={{0,1},{1,2},{2,3},{3,4},{4,5},{5,6},{6,7},{7,8},{8,9},{9,10},{10,1... | collective-permute-start | bytes 20744
  950.6 1.6 convolution_convert_fusion
  952.3 0.9 copy.16
  953.2 2.2 slice.12
  955.4 3.2 collective-permute-done.2
  958.6 6.5 concatenate
  965.1 0.7 copy.17
  (24 shorter events, 0.2 us)
Async XLA Ops:
  7.2 943.5 %copy-start = (bf16[1152,1152]{1,0:T(8,128)(2,1)S(1)}, bf16[1152,1152]{1,0:T(8,128)(2,1)}, u32[]{:S(2)}) copy-start(bf16[1152,1152]{1,0:T(8,128)(2,1)} %param.9) | copy-start | bytes 7962628
  11.7 31.7 %copy-start.4 = (s32[32,1]{0,1:T(1,128)S(1)}, s32[32,1]{0,1:T(1,128)}, u32[]{:S(2)}) copy-start(s32[32,1]{0,1:T(1,128)} %param.8) | copy-start | bytes 388
  11.7 242.9 %all-to-all-start = ((bf16[3,64,4608]{2,0,1:T(4,128)(2,1)}), bf16[3,64,4608]{2,0,1:T(4,128)(2,1)}, u32[]{:S(2)}, u32[]{:S(2)}) async-start(bf16[3,64,4608]{2,0,1:T(4,128)(2,1)} %copy.15), calls=%async_computation | async-start | bytes 4718592 | tf_op jit(solution)/shard_map/all_to_all | solution.py:22
  43.4 717.4 %all-reduce.5.cloned.1.call-start = ((), (), s32[]{:S(2)}) async-start(), calls=%async_computation.1 | async-start | bytes 10616832
  260.7 1.0 copy-start.1
  266.5 684.1 %copy-start.2 = (bf16[128,1152]{1,0:T(8,128)(2,1)}, bf16[128,1152]{1,0:T(8,128)(2,1)S(1)}, u32[]{:S(2)}) copy-start(bf16[128,1152]{1,0:T(8,128)(2,1)S(1)} %add_convert_fusion) | copy-start | bytes 884740
  892.7 59.6 %slice-start = ((bf16[3,32,4608]{2,0,1:T(4,128)(2,1)}), bf16[2,32,4608]{2,0,1:T(2,128)(2,1)S(1)}, s32[]{:S(2)}) async-start(bf16[3,32,4608]{2,0,1:T(4,128)(2,1)} %copy-done.1), calls=%async_computation.2 | async-start | bytes 1179648 | tf_op jit(solution)/shard_map/slice | solution.py:39
  892.7 42.9 %collective-permute-start.6 = (f32[36,48]{0,1:T(8,128)}, f32[36,48]{0,1:T(8,128)}, u32[]{:S(2)}, u32[]{:S(2)}) collective-permute-start(f32[36,48]{0,1:T(8,128)} %fusion), channel_id=1, source_target_pairs={{0,7},{1,8},{2,9},{3,10},{4,11},{5,12},{6,13},{7,14},{8,15},{9,16}... | collective-permute-start | bytes 20744
  894.8 44.2 %collective-permute-start.5 = (f32[36,48]{0,1:T(8,128)}, f32[36,48]{0,1:T(8,128)}, u32[]{:S(2)}, u32[]{:S(2)}) collective-permute-start(f32[36,48]{0,1:T(8,128)} %fusion), channel_id=1, source_target_pairs={{0,6},{1,7},{2,8},{3,9},{4,10},{5,11},{6,12},{7,13},{8,14},{9,15},... | collective-permute-start | bytes 20744
  899.4 34.2 %collective-permute-start.7 = (f32[36,36]{0,1:T(8,128)}, f32[36,36]{0,1:T(8,128)}, u32[]{:S(2)}, u32[]{:S(2)}) collective-permute-start(f32[36,36]{0,1:T(8,128)} %slice.17), channel_id=1, source_target_pairs={{0,8},{1,9},{2,10},{3,11},{4,12},{5,13},{6,14},{7,15},{8,16},{9,17... | collective-permute-start | bytes 15560
  907.8 47.5 %collective-permute-start.4 = (f32[36,48]{0,1:T(8,128)}, f32[36,48]{0,1:T(8,128)}, u32[]{:S(2)}, u32[]{:S(2)}) collective-permute-start(f32[36,48]{0,1:T(8,128)} %fusion), channel_id=1, source_target_pairs={{0,5},{1,6},{2,7},{3,8},{4,9},{5,10},{6,11},{7,12},{8,13},{9,14},{... | collective-permute-start | bytes 20744
  913.6 41.7 %collective-permute-start.3 = (f32[36,48]{0,1:T(8,128)}, f32[36,48]{0,1:T(8,128)}, u32[]{:S(2)}, u32[]{:S(2)}) collective-permute-start(f32[36,48]{0,1:T(8,128)} %fusion), channel_id=1, source_target_pairs={{0,4},{1,5},{2,6},{3,7},{4,8},{5,9},{6,10},{7,11},{8,12},{9,13},{1... | collective-permute-start | bytes 20744
  933.6 25.0 %collective-permute-start.2 = (f32[36,48]{0,1:T(8,128)}, f32[36,48]{0,1:T(8,128)}, u32[]{:S(2)}, u32[]{:S(2)}) collective-permute-start(f32[36,48]{0,1:T(8,128)} %fusion), channel_id=1, source_target_pairs={{0,3},{1,4},{2,5},{3,6},{4,7},{5,8},{6,9},{7,10},{8,11},{9,12},{10... | collective-permute-start | bytes 20744
  935.6 23.0 %collective-permute-start.1 = (f32[36,48]{0,1:T(8,128)}, f32[36,48]{0,1:T(8,128)}, u32[]{:S(2)}, u32[]{:S(2)}) collective-permute-start(f32[36,48]{0,1:T(8,128)} %fusion), channel_id=1, source_target_pairs={{0,2},{1,3},{2,4},{3,5},{4,6},{5,7},{6,8},{7,9},{8,10},{9,11},{10,... | collective-permute-start | bytes 20744
  939.0 19.6 %collective-permute-start = (f32[36,48]{0,1:T(8,128)}, f32[36,48]{0,1:T(8,128)}, u32[]{:S(2)}, u32[]{:S(2)}) collective-permute-start(f32[36,48]{0,1:T(8,128)} %fusion), channel_id=1, source_target_pairs={{0,1},{1,2},{2,3},{3,4},{4,5},{5,6},{6,7},{7,8},{8,9},{9,10},{10,1... | collective-permute-start | bytes 20744
  952.3 6.3 copy-start.3
Sparse Core Ops, SparseCore 0:
  271.0 489.7 all-reduce.4
where the time goes:
time: 974 us; the launch traced here: 973 us
  waiting for transfers between devices  702 us (72%)
  blocking collectives  130 us (13%)
  starting transfers between devices  86.3 us (9%)
  local copies, waits for them, and re-layouts  26.7 us (3%)
  between operations  15.5 us (2%)
    unnamed x10, waiting for transfers between devices  491 us
    all_to_all x1, waiting for transfers between devices, on_device(): lax.all_to_all(tap_slots, 'seq', split_axis=1, concat_axis=1, tiled=True)  211 us
    unnamed x1, blocking collectives  130 us
    unnamed x9, starting transfers between devices  54.6 us
    all_to_all x1, starting transfers between devices, on_device(): lax.all_to_all(tap_slots, 'seq', split_axis=1, concat_axis=1, tiled=True)  31.7 us
  transfers between devices with their start and end apart: 10, of which 3 were waited for; matrix products, arithmetic and copies ran while one was open for 1% of the time, Pallas kernels for 0%

commit v1 on v0

v1 whole, which is shorter than its diff:
```python
import functools
import math

import jax
import jax.numpy as jnp
import numpy as np
from jax import lax
from jax.experimental import pallas as pl
from jax.experimental.pallas import tpu as pltpu
from jax.sharding import Mesh
from jax.sharding import PartitionSpec as P

ZL, Y, X, ZH, C = 8, 4, 4, 4, 2
AXES = ("zl", "y", "x", "zh", "c")
MERGE = 4
M = 32
PATCHES = M * MERGE
SOURCES = X * C
SLOTS = 2 * SOURCES
BASE = 10
REST = SLOTS - BASE
KB = MERGE * BASE
KR = MERGE * REST
HELD = MERGE * ZH * 2
ROWS = SOURCES * HELD
FULL = SOURCES * MERGE * 2
TAIL = 16
GROUPS, UNIT, UPAD = 3, 12, 16
BF = jnp.bfloat16
F32 = jnp.float32


def vmem():
    return pl.BlockSpec(memory_space=pltpu.VMEM)


def smem():
    return pl.BlockSpec(memory_space=pltpu.SMEM)


def nt(a, b):
    return lax.dot_general(a, b, (((1,), (1,)), ((), ())), preferred_element_type=F32)


def nn(a, b):
    return lax.dot_general(a, b, (((1,), (0,)), ((), ())), preferred_element_type=F32)


def iota(shape, dim):
    return lax.broadcasted_iota(jnp.int32, shape, dim)


def ones_where(mask):
    return jnp.where(mask, 1.0, 0.0).astype(BF)


def like(*shape, dtype=BF):
    return jax.ShapeDtypeStruct(shape, dtype)


def call(kernel, out, *args, scratch=()):
    several = isinstance(out, list)
    return pl.pallas_call(
        kernel,
        in_specs=[smem() if a.ndim == 1 else vmem() for a in args],
        out_specs=[vmem()] * len(out) if several else vmem(),
        out_shape=out,
        scratch_shapes=scratch,
        compiler_params=pltpu.CompilerParams(vmem_limit_bytes=32 << 20),
    )(*args)


def plane(o):
    return (o >> 1) & 3


def within(o):
    return ((o >> 3) << 1) + (o & 1)


def regroup_kernel(at, in_ref, *outs):
    width = outs[0].shape[-1]
    q, s = iota((ROWS, 64), 0), iota((ROWS, 64), 1)
    x, c = ((q >> 6) + at[0]) & 3, ((q >> 5) & 1) ^ at[1]
    source = (x << 4) + (((q >> 1) & 3) << 2) + (c << 1) + (q & 1)
    total = jnp.zeros((ROWS, width), F32)
    for k in range(MERGE):
        pick = ones_where((source == s) & (((q >> 3) & 3) == k))
        total += nn(pick, in_ref[0, :, k * width : (k + 1) * width])
    total = total.astype(BF)
    if len(outs) == 1:
        outs[0][...] = total.reshape(outs[0].shape)
    else:
        for i, out in enumerate(outs):
            out[...] = total[i * HELD : (i + 1) * HELD].reshape(out.shape)


def regroup(at, tap_slots, first, levels, width, apart):
    if apart:
        out = [like(levels, HELD, width)] * SOURCES
        specs = [pl.BlockSpec((1, HELD, width), lambda i: (i, 0, 0))] * SOURCES
    else:
        out = like(SOURCES, levels, HELD, width)
        specs = pl.BlockSpec((SOURCES, 1, HELD, width), lambda i: (0, i, 0, 0))
    return pl.pallas_call(
        regroup_kernel,
        grid=(levels,),
        in_specs=[smem(), pl.BlockSpec((1, 64, MERGE * width), lambda i: (first + i, 0, 0))],
        out_specs=specs,
        out_shape=out,
    )(at, tap_slots)


def deep_kernel(held, owners, out_ref):
    q, s = iota((ROWS, ROWS), 0), iota((ROWS, ROWS), 1)
    order = (((q >> 3) & 7) << 5) + (((q >> 1) & 3) << 3) + ((q >> 6) << 1) + (q & 1)
    rows = nn(ones_where(order == s), held[...].reshape(ROWS, held.shape[-1])).astype(BF)
    for zh in range(ZH):
        for j in range(rows.shape[1] // 128):
            out_ref[zh, j * FULL : (j + 1) * FULL, :] = rows[zh * FULL : (zh + 1) * FULL, j * 128 : (j + 1) * 128]
        last = rows.shape[1] // 128 * FULL
        out_ref[zh, last : last + TAIL, :] = jnp.broadcast_to(owners[...], (TAIL, 128)).astype(BF)


def own_kernel(owners, out_ref):
    patch, token = iota((PATCHES, 128), 0), iota((PATCHES, 128), 1)
    row = jnp.broadcast_to(owners[...].astype(jnp.int32), (PATCHES, 128))
    mine = token == (patch >> 2)
    o = jnp.sum(jnp.where(mine, row, 0), axis=1, keepdims=True)
    rank = jnp.sum(jnp.where((token < (patch >> 2)) & (row == o), 1, 0), axis=1, keepdims=True)
    at = (within(o) << 3) + ((iota((PATCHES, FULL), 0) & 3) << 1) + rank
    for zh in range(ZH):
        out_ref[zh] = ones_where((plane(o) == zh) & (at == iota((PATCHES, FULL), 1)))


def stream_kernel(at, take, got, upstream, out_ref, *turned):
    tap = []
    for j in range(upstream.shape[1] // 128):
        total = nn(take[0], got[0, j * FULL : (j + 1) * FULL, :])
        for zh in range(1, ZH):
            total += nn(take[zh], got[zh, j * FULL : (j + 1) * FULL, :])
        tap.append(total)
    scratch = turned[-1]
    for j, total in enumerate(tap):
        part = (upstream[:, j * 128 : (j + 1) * 128].astype(F32) + total).astype(BF)
        out_ref[:, j * 128 : (j + 1) * 128] = part
        scratch[j * 128 : (j + 1) * 128, :] = part.astype(F32).T.astype(BF)
    rows = scratch.shape[0] // X
    for d, out in enumerate(turned[:-1]):
        first = pl.multiple_of(((at[0] + d) & 3) * rows, 32)
        out[...] = scratch[pl.ds(first, rows), :]


def list_tables():
    table = np.zeros((8, ZH * (KB + KR)), np.int32)
    for first, count, start in ((0, BASE, 0), (BASE, REST, ZH * KB)):
        q = np.arange(ZH * MERGE * count)
        at = slice(start, start + q.size)
        table[0, at] = q // (MERGE * count)
        table[1, at] = q // count % MERGE
        table[2, at] = first + q % count
    return table


def route_kernel(at, got, table_ref, column_ref, pack_base, pack_rest, take_base, take_rest, over_ref):
    tokens = ZH * M
    here = at[2]
    last = got.shape[1] - TAIL
    lane = iota((TAIL, tokens), 1) >> 5
    owners = jnp.zeros((TAIL, tokens), F32)
    for zh in range(ZH):
        owners = jnp.where(lane == zh, got[zh, last : last + TAIL, :].astype(F32), owners)
    owners = owners[0:1].astype(jnp.int32)
    t_row, t_col = iota((tokens, tokens), 1), iota((tokens, tokens), 0)
    o_row = jnp.broadcast_to(owners, (tokens, tokens))
    o_col_1 = jnp.sum(jnp.where(t_row == t_col, o_row, 0), axis=1, keepdims=True)
    o_col = jnp.broadcast_to(o_col_1, (tokens, tokens))
    mates = (t_row >> 5) == (t_col >> 5)
    listed = mates & (plane(o_row) == plane(o_col))
    s_row, s_col = within(o_row), within(o_col)
    col_before = listed & ((s_row < s_col) | ((s_row == s_col) & (t_row < t_col)))
    row_before = listed & ((s_col < s_row) | ((s_col == s_row) & (t_col < t_row)))
    place_col = jnp.sum(jnp.where(col_before, 1, 0), axis=1, keepdims=True)
    place_row = jnp.sum(jnp.where(row_before, 1, 0), axis=0, keepdims=True)
    rank_col = jnp.sum(jnp.where(mates & (o_row == o_col) & (t_row < t_col), 1, 0), axis=1, keepdims=True)
    over_ref[...] = jnp.broadcast_to(jnp.max(place_row, axis=1, keepdims=True), over_ref.shape)

    n, nb = ZH * (KB + KR), ZH * KB
    entry = ones_where(
        (column_ref[:, 0:1] == (iota((n, tokens), 1) >> 5)) & (column_ref[:, 2:3] == place_row) & (plane(owners) == here)
    )
    row = iota((tokens, HELD), 1)
    held = (((row >> 1) & 3) == (iota((tokens, HELD), 0) >> 5)) & ((row & 1) == rank_col)
    same_k = column_ref[:, 1:2] == (iota((n, HELD), 1) >> 3)
    for source in range(SOURCES):
        pick = nn(entry, ones_where(held & (within(o_col_1) == source)))
        pick = jnp.where(same_k, pick, 0.0).astype(BF)
        pack_base[source] = pick[:nb]
        pack_rest[source] = pick[nb:]
    mine = ones_where(iota((PATCHES, tokens), 1) == here * M + (iota((PATCHES, tokens), 0) >> 2))

    def take(zh, first, count):
        q = table_ref[:, first : first + count]
        taken = nn(mine, ones_where((plane(o_col_1) == zh) & (q[2:3, :] == place_col)))
        return jnp.where(q[1:2, :] == (iota((PATCHES, count), 0) & 3), taken, 0.0).astype(BF)

    for zh in range(ZH):
        take_base[zh] = take(zh, zh * KB, KB)
        take_rest[zh] = take(zh, nb + zh * KR, KR)


def route(at, got):
    table = list_tables()
    out = [
        like(SOURCES, ZH * KB, HELD),
        like(SOURCES, ZH * KR, HELD),
        like(ZH, PATCHES, KB),
        like(ZH, PATCHES, KR),
        like(8, 128, dtype=jnp.int32),
    ]
    return call(route_kernel, out, at, got, jnp.asarray(table), jnp.asarray(table.T))


def pack_kernel(level, at, picks, *refs):
    held, out = refs[:-1], refs[-1]
    total = None
    for i, ref in enumerate(held):
        source = (((at[0] - (i >> 1)) & 3) << 1) + ((i & 1) ^ at[1])
        part = nn(picks[source], ref[level])
        total = part if total is None else total + part
    rows = out.shape[1]
    for zh in range(ZH):
        out[zh] = total[zh * rows : (zh + 1) * rows].astype(BF)


def pack(at, picks, held, level):
    out = like(ZH, picks.shape[1] // ZH, held[0].shape[-1])
    return call(functools.partial(pack_kernel, level), out, at, picks, *held)


def shallow_kernel(take_base, take_rest, got0, got1, rest, out_ref):
    width = out_ref.shape[-1]
    for level, got in enumerate((got0, got1)):
        tap = jnp.zeros((PATCHES, width), F32)
        for zh in range(ZH):
            tap += nn(take_base[zh], got[zh, :, :width])
            tap += nn(take_rest[zh], rest[level, zh])
        out_ref[level] = tap.astype(BF)


def partial_kernel(at, a0, a1, a2, a3, s0, s1, s2, s3, place, mine, other, scratch):
    total = nt(a0[...], s0[...])
    for a, s in ((a1, s1), (a2, s2), (a3, s3)):
        total += nt(a[...], s[...])
    scratch[...] = total.astype(BF)
    rows = ZL * UPAD
    for d in range(Y):
        y = (at[3] + d) & 3
        block = None
        for g in range(GROUPS):
            first = pl.multiple_of((y * GROUPS + g) * rows, rows)
            part = nn(scratch[pl.ds(first, rows), :], place[g])
            block = part if block is None else block + part
        low, high = block[:, : ZH * 128], block[:, ZH * 128 :]
        first_core = at[1] == 0
        ours, theirs = jnp.where(first_core, low, high), jnp.where(first_core, high, low)
        for zh in range(ZH):
            mine[d, zh] = ours[:, zh * 128 : (zh + 1) * 128]
            other[d, zh] = theirs[:, zh * 128 : (zh + 1) * 128].astype(BF)


def sum_c_kernel(mine, got, own, *outs):
    own[...] = mine[0] + got[0].astype(F32)
    for d, out in enumerate(outs, 1):
        out[...] = (mine[d] + got[d].astype(F32)).astype(BF)


def sum_y_kernel(own, g1, g2, g3, out_ref):
    total = own[...] + g1[...].astype(F32) + g2[...].astype(F32) + g3[...].astype(F32)
    for zl in range(ZL):
        out_ref[zl] = total[:, zl * UPAD : (zl + 1) * UPAD, :].astype(BF)


def join_kernel(parts, rows, out_ref):
    width = rows.shape[-1]
    total = parts[0].astype(F32)
    for i in range(1, ZL):
        total += parts[i].astype(F32)
    out_ref[:, :, :width] = rows[...]
    out_ref[:, :UPAD, width:] = total.astype(BF)
    out_ref[:, UPAD:, width:] = jnp.zeros((ZH, rows.shape[1] - UPAD, 128), BF)


def final_kernel(factor, got, out_ref):
    width = got.shape[-1] - 128
    total = got[0, :UPAD, width:].astype(F32)
    for i in range(1, ZH):
        total += got[i, :UPAD, width:].astype(F32)
    total = total * factor
    for g in range(GROUPS):
        out_ref[g * UNIT : (g + 1) * UNIT, :] = total[:UNIT, g * 36 : (g + 1) * 36]


def after(x, *earlier):
    return lax.optimization_barrier((x, *earlier))[0]


def exchange(x, axes):
    return lax.all_to_all(x, axes, 0, 0, tiled=True)


def shift(x, axis, by):
    n = lax.axis_size(axis)
    return lax.ppermute(x, axis, [(i, (i + by) % n) for i in range(n)])


def shift_xc(x, i):
    dx, dc = i >> 1, i & 1
    return lax.ppermute(x, ("x", "c"), [(a * C + b, (a + dx) % X * C + (b ^ dc)) for a in range(X) for b in range(C)])


def on_device(attention_out, upstream, tap_slots, owner_map, out_proj):
    width = attention_out.shape[1]
    factor = 1.0 / math.sqrt(PATCHES * ZL * Y * X * ZH * C)
    at = jnp.stack([lax.axis_index(a) for a in ("x", "c", "zh", "y")]).astype(jnp.int32)
    owners = jnp.tile(owner_map.reshape(1, M), (1, ZH)).astype(F32)

    q = np.arange(Y * GROUPS * ZL * UPAD)
    u, zl, g, y = q % UPAD, q // UPAD % ZL, q // (UPAD * ZL) % GROUPS, q // (UPAD * ZL * GROUPS)
    r_of = np.where(u < UNIT, zl * 144 + y * 36 + g * UNIT + u, -1)
    select = (jnp.asarray(r_of, jnp.int32)[:, None] == jnp.arange(width, dtype=jnp.int32)[None, :]).astype(BF)
    a_t = nt(select, attention_out).astype(BF)
    i, n = np.arange(288)[:, None], np.arange(C * ZH * 128)[None, :]
    j = [n % 128 - 36 * g for g in range(GROUPS)]
    place = np.stack([(i == (n // 128 % ZH) * 72 + (n // 512) * 36 + e) & (e >= 0) & (e < 36) for e in j])
    place = jnp.asarray(place.astype(np.float32), BF)

    held2 = exchange(regroup(jnp.zeros((4,), jnp.int32), tap_slots, 2, 1, width, False), ("x", "c"))
    take2 = call(own_kernel, like(ZH, PATCHES, FULL), owners)
    got2 = exchange(call(deep_kernel, like(ZH, width // 128 * FULL + TAIL, 128), held2, owners), "zh")
    held01 = [after(part, held2) for part in regroup(at, tap_slots, 0, 2, width, True)]
    held01 = [held01[0]] + [shift_xc(part, i) for i, part in enumerate(held01) if i]
    a_t = after(a_t, held2)
    a_from = [a_t] + [shift(a_t, "x", d) for d in (1, 2, 3)]

    pack_base, pack_rest, take_base, take_rest, over = route(after(at, take2, *a_from), got2)
    overflow = over[0, 0] >= BASE
    got0 = exchange(pack(at, pack_base, held01, 0), "zh")
    packed1 = pack(at, pack_base, held01, 1)

    turned = [like(width // X, PATCHES)] * X
    stream, *turned = call(
        stream_kernel, [like(PATCHES, width), *turned], at, take2, got2, upstream, scratch=[pltpu.VMEM((width, PATCHES), BF)]
    )
    s_from = [turned[0]] + [shift(turned[d], "x", d) for d in (1, 2, 3)]
    attention_grad = nt(stream, out_proj).astype(BF)
    block = (Y, ZH, ZL * UPAD, 128)
    mine, other = call(
        partial_kernel,
        [like(*block, dtype=F32), like(*block)],
        at,
        *a_from,
        *s_from,
        place,
        scratch=[pltpu.VMEM((a_t.shape[0], width // X), BF)],
    )
    own, *parts = call(sum_c_kernel, [like(*block[1:], dtype=F32)] + [like(*block[1:])] * 3, mine, shift(other, "c", 1))
    parts = [shift(part, "y", d) for d, part in enumerate(parts, 1)]
    partial = call(sum_y_kernel, like(ZL, ZH, UPAD, 128), own, *parts)
    partial = exchange(after(partial, got0), "zl")
    got1 = exchange(call(join_kernel, like(ZH, KB, width + 128), partial, packed1), "zh")
    proj_grad = call(functools.partial(final_kernel, factor), like(36, 36, dtype=F32), got1)

    def second(picks, *held):
        return jnp.stack([exchange(pack(at, picks, held, level), "zh") for level in (0, 1)])

    rest = lax.cond(
        overflow, second, lambda picks, *held: jnp.zeros((2, ZH, KR, width), BF), after(pack_rest, got1), *held01
    )
    shallow = call(shallow_kernel, like(2, PATCHES, width), take_base, take_rest, got0, got1, rest)
    return (stream, attention_grad, shallow, proj_grad)


def solution(mesh):
    fine = Mesh(mesh.devices.reshape(ZL, Y, X, ZH, C), AXES)
    dp, seq = ("zl", "y"), ("x", "zh", "c")
    in_specs = (P(AXES, None), P(AXES, None), P(None, AXES, None), P(AXES, None), P())
    out_specs = (P(AXES, None), P(AXES, None), P(None, AXES, None), P(dp, seq))
    return jax.shard_map(on_device, mesh=fine, in_specs=in_specs, out_specs=out_specs, check_vma=False)
```

time: 974 us -> 263 us (0.27)
  the two profiles are of different devices: /device:TPU:2 before, /device:TPU:41 now
where the time goes in v1:
time: 263 us; the launch traced here: 262 us
  starting transfers between devices  119 us (45%)
  waiting for transfers between devices  102 us (39%)
  Pallas kernels  25.8 us (10%)
  local copies, waits for them, and re-layouts  7.99 us (3%)
  matrix products  5.71 us (2%)
    all_to_all x5, waiting for transfers between devices, exchange(): return lax.all_to_all(x, axes, 0, 0, tiled=True)  85.6 us
    all_to_all x5, starting transfers between devices, exchange(): return lax.all_to_all(x, axes, 0, 0, tiled=True)  66.7 us
    ppermute x10, starting transfers between devices, shift(): return lax.ppermute(x, axis, [(i, (i + by) % n) for i in range(n)])  29.9 us
    ppermute x7, starting transfers between devices, shift_xc(): lax.ppermute(x, ('x', 'c'), [(a * C + b, (a + dx) % X * C + (b ^ dc)) for...  22.1 us
    pallas_call x12, Pallas kernels, call(): pl.pallas_call(kernel, in_specs=[smem() if a.ndim == 1 else vmem() for a...  19.6 us
    ppermute x10, waiting for transfers between devices, shift(): return lax.ppermute(x, axis, [(i, (i + by) % n) for i in range(n)])  9.97 us
    pallas_call x2, Pallas kernels, regroup(): pl.pallas_call(regroup_kernel, grid=(levels,), in_specs=[smem(), pl.Block...  6.26 us
    ppermute x7, waiting for transfers between devices, shift_xc(): lax.ppermute(x, ('x', 'c'), [(a * C + b, (a + dx) % X * C + (b ^ dc)) for...  6.08 us
  transfers between devices with their start and end apart: 22, of which 10 were waited for; matrix products, arithmetic and copies ran while one was open for 2% of the time, Pallas kernels for 6%

profile of v1, /device:TPU:41, one launch (start us, length us, event | category | flops | bytes accessed | tf_op | source)
XLA Modules:
  0.0 261.6 jit_solution(8412148737192701606)
XLA Ops:
  1.2 2.8 %shard_map.121 = bf16[8,1,32,1152]{3,2,1,0:T(8,128)(2,1)} custom-call(s32[4]{0:T(128)} %broadcast_3_at.2.at, bf16[3,64,4608]{2,1,0:T(8,128)(2,1)} %in_ref.3), custom_call_target="tpu_custom_call" | custom-call | tf_op jit(solution)/shard_map/pallas_call | solution.py:105
  3.9 5.0 %all-to-all-start.2 = ((bf16[8,1,32,1152]{3,2,1,0:T(8,128)(2,1)}), bf16[8,1,32,1152]{3,2,1,0:T(8,128)(2,1)S(1)}, u32[]{:S(2)}, u32[]{:S(2)}) async-start(bf16[8,1,32,1152]{3,2,1,0:T(8,128)(2,1)} %shard_map.121), calls=%async_computation.2 | async-start | bytes 1179648 | tf_op jit(solution)/shard_map/all_to_all | solution.py:309
  9.0 10.1 %all-to-all-done.2.held = bf16[8,1,32,1152]{3,2,1,0:T(8,128)(2,1)S(1)} async-done(((bf16[8,1,32,1152]{3,2,1,0:T(8,128)(2,1)}), bf16[8,1,32,1152]{3,2,1,0:T(8,128)(2,1)S(1)}, u32[]{:S(2)}, u32[]{:S(2)}) %all-to-all-start.2) | async-done | bytes 589856 | tf_op jit(solution)/shard_map/all_to_all | solution.py:309
  20.3 27.2 %all-to-all-start.3 = ((bf16[4,592,128]{2,1,0:T(8,128)(2,1)}), bf16[4,592,128]{2,1,0:T(8,128)(2,1)S(1)}, u32[]{:S(2)}, u32[]{:S(2)}) async-start(bf16[4,592,128]{2,1,0:T(8,128)(2,1)} %copy-done.1), calls=%async_computation.3 | async-start | bytes 1212416 | tf_op jit(solution)/shard_map/all_to_all | solution.py:309
  47.4 3.1 %fusion.2.a0 = bf16[1536,128]{1,0:T(8,128)(2,1)} fusion(bf16[128,1152]{1,0:T(8,128)(2,1)} %param.11, s32[1536]{0:T(1024)S(1)} %copy-done.18), kind=kOutput, calls=%fused_computation.4 | convolution fusion | flops 454950912 | bytes 694272 | tf_op jit(solution)/shard_map/dot_general | solution.py:42
  50.6 2.8 %collective-permute-start.2 = (bf16[1536,128]{1,0:T(8,128)(2,1)}, bf16[1536,128]{1,0:T(8,128)(2,1)}, u32[]{:S(2)}, u32[]{:S(2)}) collective-permute-start(bf16[1536,128]{1,0:T(8,128)(2,1)} %fusion.2.a0), channel_id=1, source_target_pairs={{0,24},{8,0},{16,8},{24,16},{1,25},{9,1},{17,9},{25,17},{2,26},{10... | collective-permute-start | bytes 1179656 | tf_op jit(solution)/shard_map/ppermute | solution.py:314
  53.3 3.1 %collective-permute-start.1 = (bf16[1536,128]{1,0:T(8,128)(2,1)}, bf16[1536,128]{1,0:T(8,128)(2,1)}, u32[]{:S(2)}, u32[]{:S(2)}) collective-permute-start(bf16[1536,128]{1,0:T(8,128)(2,1)} %fusion.2.a0), channel_id=1, source_target_pairs={{0,16},{8,24},{16,0},{24,8},{1,17},{9,25},{17,1},{25,9},{2,18},{10... | collective-permute-start | bytes 1179656 | tf_op jit(solution)/shard_map/ppermute | solution.py:314
  58.5 3.5 %shard_map.125 = (bf16[2,32,1152]{2,1,0:T(8,128)(2,1)}, bf16[2,32,1152]{2,1,0:T(8,128)(2,1)}, bf16[2,32,1152]{2,1,0:T(8,128)(2,1)}, bf16[2,32,1152]{2,1,0:T(8,12...) custom-call(s32[4]{0:T(128)S(1)} %pad_add_fusion.at, ...), custom_call_target="tpu_custom_call" | custom-call | tf_op jit(solution)/shard_map/pallas_call | solution.py:105
  62.0 6.4 %collective-permute-start.9 = (bf16[2,32,1152]{2,1,0:T(8,128)(2,1)}, bf16[2,32,1152]{2,1,0:T(8,128)(2,1)S(1)}, u32[]{:S(2)}, u32[]{:S(2)}) collective-permute-start(bf16[2,32,1152]{2,1,0:T(8,128)(2,1)} %get-tuple-element.94), channel_id=1, source_target_pairs={{0,25},{1,24},{8,1},{9,0},{16,9},{17,8},{24,17},{25,16},{2,27},{3,... | collective-permute-start | bytes 442376 | tf_op jit(solution)/shard_map/ppermute | solution.py:319
  68.4 2.5 collective-permute-start.8
  70.9 6.1 %collective-permute-done.9.refs_7_ = bf16[2,32,1152]{2,1,0:T(8,128)(2,1)S(1)} collective-permute-done((bf16[2,32,1152]{2,1,0:T(8,128)(2,1)}, bf16[2,32,1152]{2,1,0:T(8,128)(2,1)S(1)}, u32[]{:S(2)}, u32[]{:S(2)}) %collective-permute-start.9) | collective-permute-done | bytes 147488 | tf_op jit(solution)/shard_map/ppermute | solution.py:319
  78.9 2.4 collective-permute-start.6
  81.3 4.5 %collective-permute-start.5 = (bf16[2,32,1152]{2,1,0:T(8,128)(2,1)}, bf16[2,32,1152]{2,1,0:T(8,128)(2,1)}, u32[]{:S(2)}, u32[]{:S(2)}) collective-permute-start(bf16[2,32,1152]{2,1,0:T(8,128)(2,1)} %get-tuple-element.86), channel_id=1, source_target_pairs={{0,9},{1,8},{8,17},{9,16},{16,25},{17,24},{24,1},{25,0},{2,11},{3,... | collective-permute-start | bytes 442376 | tf_op jit(solution)/shard_map/ppermute | solution.py:319
  85.8 2.4 collective-permute-start.4
  90.5 23.3 %all-to-all-done.3.got = bf16[4,592,128]{2,1,0:T(8,128)(2,1)S(1)} async-done(((bf16[4,592,128]{2,1,0:T(8,128)(2,1)}), bf16[4,592,128]{2,1,0:T(8,128)(2,1)S(1)}, u32[]{:S(2)}, u32[]{:S(2)}) %all-to-all-start.3) | async-done | bytes 606240 | tf_op jit(solution)/shard_map/all_to_all | solution.py:309
  117.1 2.2 shard_map.126
  120.8 7.2 %all-to-all-start.4 = ((bf16[4,40,1152]{2,1,0:T(8,128)(2,1)}), bf16[4,40,1152]{2,1,0:T(8,128)(2,1)}, u32[]{:S(2)}, u32[]{:S(2)}) async-start(bf16[4,40,1152]{2,1,0:T(8,128)(2,1)} %copy-done.3), calls=%async_computation.4 | async-start | bytes 737280 | tf_op jit(solution)/shard_map/all_to_all | solution.py:309
  132.9 3.7 %collective-permute-start.11 = (bf16[288,128]{1,0:T(8,128)(2,1)S(1)}, bf16[288,128]{1,0:T(8,128)(2,1)S(1)}, u32[]{:S(2)}, u32[]{:S(2)}) collective-permute-start(bf16[288,128]{1,0:T(8,128)(2,1)S(1)} %get-tuple-element.97), channel_id=1, source_target_pairs={{0,16},{8,24},{16,0},{24,8},{1,17},{9,25},{17,1},{25,9},{2,18},{10... | collective-permute-start | bytes 221192 | tf_op jit(solution)/shard_map/ppermute | solution.py:314
  136.6 2.5 collective-permute-start.12
  139.6 3.2 %collective-permute-done.12.s3 = bf16[288,128]{1,0:T(8,128)(2,1)S(1)} collective-permute-done((bf16[288,128]{1,0:T(8,128)(2,1)S(1)}, bf16[288,128]{1,0:T(8,128)(2,1)S(1)}, u32[]{:S(2)}, u32[]{:S(2)}) %collective-permute-start.12) | collective-permute-done | bytes 73760 | tf_op jit(solution)/shard_map/ppermute | solution.py:314
  144.2 5.3 %shard_map.127 = (f32[4,4,128,128]{3,2,1,0:T(8,128)S(1)}, bf16[4,4,128,128]{3,2,1,0:T(8,128)(2,1)S(1)}) custom-call(s32[4]{0:T(128)S(1)} %pad_add_fusion.at, bf16[1536,128]{1,0:T(8,128)(2,1)} %fusion.2.a0, bf16[1536,128]{1,0:T(8,128)(2,1)} %collective-permute-done.a1, bf16[1536,128]{1,0:T(8,128)(2,1)} %collective-permute-done.1.a2, ...), custom_call_target="tpu_custom_call" | custom-call | tf_op jit(solution)/shard_map/pallas_call | solution.py:63
  149.6 3.9 %collective-permute-start.13 = (bf16[4,4,128,128]{3,2,1,0:T(8,128)(2,1)S(1)}, bf16[4,4,128,128]{3,2,1,0:T(8,128)(2,1)S(1)}, u32[]{:S(2)}, u32[]{:S(2)}) collective-permute-start(bf16[4,4,128,128]{3,2,1,0:T(8,128)(2,1)S(1)} %get-tuple-element.100), channel_id=1, source_target_pairs={{0,1},{1,0},{2,3},{3,2},{4,5},{5,4},{6,7},{7,6},{8,9},{9,8},{10,11... | collective-permute-start | bytes 1572872 | tf_op jit(solution)/shard_map/ppermute | solution.py:314
  155.1 3.2 %collective-permute-start.14 = (bf16[4,128,128]{2,1,0:T(8,128)(2,1)S(1)}, bf16[4,128,128]{2,1,0:T(8,128)(2,1)S(1)}, u32[]{:S(2)}, u32[]{:S(2)}) collective-permute-start(bf16[4,128,128]{2,1,0:T(8,128)(2,1)S(1)} %get-tuple-element.102), channel_id=1, source_target_pairs={{0,32},{32,64},{64,96},{96,0},{1,33},{33,65},{65,97},{97,1},{2,34}... | collective-permute-start | bytes 393224 | tf_op jit(solution)/shard_map/ppermute | solution.py:314
  158.3 2.6 %collective-permute-start.15 = (bf16[4,128,128]{2,1,0:T(8,128)(2,1)S(1)}, bf16[4,128,128]{2,1,0:T(8,128)(2,1)S(1)}, u32[]{:S(2)}, u32[]{:S(2)}) collective-permute-start(bf16[4,128,128]{2,1,0:T(8,128)(2,1)S(1)} %get-tuple-element.103), channel_id=1, source_target_pairs={{0,64},{32,96},{64,0},{96,32},{1,65},{33,97},{65,1},{97,33},{2,66}... | collective-permute-start | bytes 393224 | tf_op jit(solution)/shard_map/ppermute | solution.py:314
  160.9 4.0 %collective-permute-start.16 = (bf16[4,128,128]{2,1,0:T(8,128)(2,1)S(1)}, bf16[4,128,128]{2,1,0:T(8,128)(2,1)S(1)}, u32[]{:S(2)}, u32[]{:S(2)}) collective-permute-start(bf16[4,128,128]{2,1,0:T(8,128)(2,1)S(1)} %get-tuple-element.104), channel_id=1, source_target_pairs={{0,96},{32,0},{64,32},{96,64},{1,97},{33,1},{65,33},{97,65},{2,98}... | collective-permute-start | bytes 393224 | tf_op jit(solution)/shard_map/ppermute | solution.py:314
  166.2 3.5 %collective-permute-done.16.g3 = bf16[4,128,128]{2,1,0:T(8,128)(2,1)S(1)} collective-permute-done((bf16[4,128,128]{2,1,0:T(8,128)(2,1)S(1)}, bf16[4,128,128]{2,1,0:T(8,128)(2,1)S(1)}, u32[]{:S(2)}, u32[]{:S(2)}) %collective-permute-start.16) | collective-permute-done | bytes 131104 | tf_op jit(solution)/shard_map/ppermute | solution.py:314
  170.4 6.0 %all-to-all-start.5 = ((bf16[8,4,16,128]{3,2,1,0:T(8,128)(2,1)}), bf16[8,4,16,128]{3,2,1,0:T(8,128)(2,1)S(1)}, u32[]{:S(2)}, u32[]{:S(2)}) async-start(bf16[8,4,16,128]{3,2,1,0:T(8,128)(2,1)} %shard_map.129), calls=%async_computation.5 | async-start | bytes 262144 | tf_op jit(solution)/shard_map/all_to_all | solution.py:309
  178.7 6.5 %all-to-all-done.5.parts = bf16[8,4,16,128]{3,2,1,0:T(8,128)(2,1)S(1)} async-done(((bf16[8,4,16,128]{3,2,1,0:T(8,128)(2,1)}), bf16[8,4,16,128]{3,2,1,0:T(8,128)(2,1)S(1)}, u32[]{:S(2)}, u32[]{:S(2)}) %all-to-all-start.5) | async-done | bytes 131104 | tf_op jit(solution)/shard_map/all_to_all | solution.py:309
  186.0 21.3 %all-to-all-start.6 = ((bf16[4,40,1280]{2,1,0:T(8,128)(2,1)}), bf16[4,40,1280]{2,1,0:T(8,128)(2,1)S(1)}, u32[]{:S(2)}, u32[]{:S(2)}) async-start(bf16[4,40,1280]{2,1,0:T(8,128)(2,1)} %shard_map.131), calls=%async_computation.6 | async-start | bytes 819200 | tf_op jit(solution)/shard_map/all_to_all | solution.py:309
  208.5 2.6 convolution_convert_fusion
  211.1 45.8 %all-to-all-done.6.got1.got = bf16[4,40,1280]{2,1,0:T(8,128)(2,1)S(1)} async-done(((bf16[4,40,1280]{2,1,0:T(8,128)(2,1)}), bf16[4,40,1280]{2,1,0:T(8,128)(2,1)S(1)}, u32[]{:S(2)}, u32[]{:S(2)}) %all-to-all-start.6) | async-done | bytes 409632 | tf_op jit(solution)/shard_map/all_to_all | solution.py:309
  258.3 3.3 %shard_map.132 = bf16[2,128,1152]{2,1,0:T(8,128)(2,1)} custom-call(bf16[4,128,40]{2,1,0:T(8,128)(2,1)S(1)} %copy-done.8, bf16[4,128,24]{2,1,0:T(8,128)(2,1)S(1)} %copy-done.10, bf16[4,40,1152]{2,1,0:T(8,128)(2,1)} %all-to-all-done.4.got0, bf16[4,40,1280]{2,1,0:T(8,128)(2,1)S(1)} %all-to-all-done.6.got1.got, bf16[2,4,24,1152]{3,2,1,0:T(8,128)(2,1)} %get-tuple-element.109.rest), custom_call_target="tpu_custom_call" | custom-call | tf_op jit(solution)/shard_map/pallas_call | solution.py:63
  (72 shorter events, 28.9 us)
Async XLA Ops:
  0.6 207.8 %copy-start = (bf16[1152,1152]{1,0:T(8,128)(2,1)S(1)}, bf16[1152,1152]{1,0:T(8,128)(2,1)}, u32[]{:S(2)}) copy-start(bf16[1152,1152]{1,0:T(8,128)(2,1)} %param.15) | copy-start | bytes 7962628
  0.6 8.3 %copy-start.17 = (s32[32,1]{0,1:T(1,128)S(1)}, s32[32,1]{0,1:T(1,128)}, u32[]{:S(2)}) copy-start(s32[32,1]{0,1:T(1,128)} %param.14) | copy-start | bytes 388
  1.2 46.3 %copy-start.18 = (s32[1536]{0:T(1024)S(1)}, s32[1536]{0:T(1024)}, u32[]{:S(2)}) copy-start(s32[1536]{0:T(1024)} %constant.30.clone) | copy-start | bytes 18436
  3.9 15.1 %all-to-all-start.2 = ((bf16[8,1,32,1152]{3,2,1,0:T(8,128)(2,1)}), bf16[8,1,32,1152]{3,2,1,0:T(8,128)(2,1)S(1)}, u32[]{:S(2)}, u32[]{:S(2)}) async-start(bf16[8,1,32,1152]{3,2,1,0:T(8,128)(2,1)} %shard_map.121), calls=%async_computation.2 | async-start | bytes 1179648 | tf_op jit(solution)/shard_map/all_to_all | solution.py:309
  20.3 93.5 %all-to-all-start.3 = ((bf16[4,592,128]{2,1,0:T(8,128)(2,1)}), bf16[4,592,128]{2,1,0:T(8,128)(2,1)S(1)}, u32[]{:S(2)}, u32[]{:S(2)}) async-start(bf16[4,592,128]{2,1,0:T(8,128)(2,1)} %copy-done.1), calls=%async_computation.3 | async-start | bytes 1212416 | tf_op jit(solution)/shard_map/all_to_all | solution.py:309
  47.4 66.4 %copy-start.11 = (s32[256,8]{1,0:T(8,128)S(1)}, s32[256,8]{1,0:T(8,128)}, u32[]{:S(2)}) copy-start(s32[256,8]{1,0:T(8,128)} %constant.33.clone.column_ref) | copy-start | bytes 24580
  47.4 66.4 %copy-start.12 = (s32[8,256]{1,0:T(8,128)S(1)}, s32[8,256]{1,0:T(8,128)}, u32[]{:S(2)}) copy-start(s32[8,256]{1,0:T(8,128)} %constant.32.clone.table_ref) | copy-start | bytes 24580
  50.6 30.8 %collective-permute-start.2 = (bf16[1536,128]{1,0:T(8,128)(2,1)}, bf16[1536,128]{1,0:T(8,128)(2,1)}, u32[]{:S(2)}, u32[]{:S(2)}) collective-permute-start(bf16[1536,128]{1,0:T(8,128)(2,1)} %fusion.2.a0), channel_id=1, source_target_pairs={{0,24},{8,0},{16,8},{24,16},{1,25},{9,1},{17,9},{25,17},{2,26},{10... | collective-permute-start | bytes 1179656 | tf_op jit(solution)/shard_map/ppermute | solution.py:314
  53.3 32.5 %collective-permute-start.1 = (bf16[1536,128]{1,0:T(8,128)(2,1)}, bf16[1536,128]{1,0:T(8,128)(2,1)}, u32[]{:S(2)}, u32[]{:S(2)}) collective-permute-start(bf16[1536,128]{1,0:T(8,128)(2,1)} %fusion.2.a0), channel_id=1, source_target_pairs={{0,16},{8,24},{16,0},{24,8},{1,17},{9,25},{17,1},{25,9},{2,18},{10... | collective-permute-start | bytes 1179656 | tf_op jit(solution)/shard_map/ppermute | solution.py:314
  56.4 31.8 %collective-permute-start = (bf16[1536,128]{1,0:T(8,128)(2,1)}, bf16[1536,128]{1,0:T(8,128)(2,1)}, u32[]{:S(2)}, u32[]{:S(2)}) collective-permute-start(bf16[1536,128]{1,0:T(8,128)(2,1)} %fusion.2.a0), channel_id=1, source_target_pairs={{0,8},{8,16},{16,24},{24,0},{1,9},{9,17},{17,25},{25,1},{2,10},{10... | collective-permute-start | bytes 1179656 | tf_op jit(solution)/shard_map/ppermute | solution.py:314
  62.0 15.0 %collective-permute-start.9 = (bf16[2,32,1152]{2,1,0:T(8,128)(2,1)}, bf16[2,32,1152]{2,1,0:T(8,128)(2,1)S(1)}, u32[]{:S(2)}, u32[]{:S(2)}) collective-permute-start(bf16[2,32,1152]{2,1,0:T(8,128)(2,1)} %get-tuple-element.94), channel_id=1, source_target_pairs={{0,25},{1,24},{8,1},{9,0},{16,9},{17,8},{24,17},{25,16},{2,27},{3,... | collective-permute-start | bytes 442376 | tf_op jit(solution)/shard_map/ppermute | solution.py:319
  68.4 10.5 %collective-permute-start.8 = (bf16[2,32,1152]{2,1,0:T(8,128)(2,1)}, bf16[2,32,1152]{2,1,0:T(8,128)(2,1)S(1)}, u32[]{:S(2)}, u32[]{:S(2)}) collective-permute-start(bf16[2,32,1152]{2,1,0:T(8,128)(2,1)} %get-tuple-element.92), channel_id=1, source_target_pairs={{0,24},{1,25},{8,0},{9,1},{16,8},{17,9},{24,16},{25,17},{2,26},{3,... | collective-permute-start | bytes 442376 | tf_op jit(solution)/shard_map/ppermute | solution.py:319
  77.0 11.3 %copy-start.15 = (bf16[2,32,1152]{2,1,0:T(8,128)(2,1)}, bf16[2,32,1152]{2,1,0:T(8,128)(2,1)S(1)}, u32[]{:S(2)}) copy-start(bf16[2,32,1152]{2,1,0:T(8,128)(2,1)S(1)} %collective-permute-done.9.refs_7_) | copy-start | bytes 442372
  77.0 40.0 %collective-permute-start.7 = (bf16[2,32,1152]{2,1,0:T(8,128)(2,1)}, bf16[2,32,1152]{2,1,0:T(8,128)(2,1)}, u32[]{:S(2)}, u32[]{:S(2)}) collective-permute-start(bf16[2,32,1152]{2,1,0:T(8,128)(2,1)} %get-tuple-element.90), channel_id=1, source_target_pairs={{0,17},{1,16},{8,25},{9,24},{16,1},{17,0},{24,9},{25,8},{2,19},{3,... | collective-permute-start | bytes 442376 | tf_op jit(solution)/shard_map/ppermute | solution.py:319
  78.9 9.4 %copy-start.16 = (bf16[2,32,1152]{2,1,0:T(8,128)(2,1)}, bf16[2,32,1152]{2,1,0:T(8,128)(2,1)S(1)}, u32[]{:S(2)}) copy-start(bf16[2,32,1152]{2,1,0:T(8,128)(2,1)S(1)} %collective-permute-done.8.refs_6_) | copy-start | bytes 442372
  78.9 38.1 %collective-permute-start.6 = (bf16[2,32,1152]{2,1,0:T(8,128)(2,1)}, bf16[2,32,1152]{2,1,0:T(8,128)(2,1)}, u32[]{:S(2)}, u32[]{:S(2)}) collective-permute-start(bf16[2,32,1152]{2,1,0:T(8,128)(2,1)} %get-tuple-element.88), channel_id=1, source_target_pairs={{0,16},{1,17},{8,24},{9,25},{16,0},{17,1},{24,8},{25,9},{2,18},{3,... | collective-permute-start | bytes 442376 | tf_op jit(solution)/shard_map/ppermute | solution.py:319
  81.3 35.7 %collective-permute-start.5 = (bf16[2,32,1152]{2,1,0:T(8,128)(2,1)}, bf16[2,32,1152]{2,1,0:T(8,128)(2,1)}, u32[]{:S(2)}, u32[]{:S(2)}) collective-permute-start(bf16[2,32,1152]{2,1,0:T(8,128)(2,1)} %get-tuple-element.86), channel_id=1, source_target_pairs={{0,9},{1,8},{8,17},{9,16},{16,25},{17,24},{24,1},{25,0},{2,11},{3,... | collective-permute-start | bytes 442376 | tf_op jit(solution)/shard_map/ppermute | solution.py:319
  85.8 31.2 %collective-permute-start.4 = (bf16[2,32,1152]{2,1,0:T(8,128)(2,1)}, bf16[2,32,1152]{2,1,0:T(8,128)(2,1)}, u32[]{:S(2)}, u32[]{:S(2)}) collective-permute-start(bf16[2,32,1152]{2,1,0:T(8,128)(2,1)} %get-tuple-element.84), channel_id=1, source_target_pairs={{0,8},{1,9},{8,16},{9,17},{16,24},{17,25},{24,0},{25,1},{2,10},{3,... | collective-permute-start | bytes 442376 | tf_op jit(solution)/shard_map/ppermute | solution.py:319
  88.3 28.8 %collective-permute-start.3 = (bf16[2,32,1152]{2,1,0:T(8,128)(2,1)}, bf16[2,32,1152]{2,1,0:T(8,128)(2,1)}, u32[]{:S(2)}, u32[]{:S(2)}) collective-permute-start(bf16[2,32,1152]{2,1,0:T(8,128)(2,1)} %get-tuple-element.82), channel_id=1, source_target_pairs={{0,1},{1,0},{8,9},{9,8},{16,17},{17,16},{24,25},{25,24},{2,3},{3,2... | collective-permute-start | bytes 442376 | tf_op jit(solution)/shard_map/ppermute | solution.py:319
  120.8 49.7 %all-to-all-start.4 = ((bf16[4,40,1152]{2,1,0:T(8,128)(2,1)}), bf16[4,40,1152]{2,1,0:T(8,128)(2,1)}, u32[]{:S(2)}, u32[]{:S(2)}) async-start(bf16[4,40,1152]{2,1,0:T(8,128)(2,1)} %copy-done.3), calls=%async_computation.4 | async-start | bytes 737280 | tf_op jit(solution)/shard_map/all_to_all | solution.py:309
  130.7 8.4 %collective-permute-start.10 = (bf16[288,128]{1,0:T(8,128)(2,1)S(1)}, bf16[288,128]{1,0:T(8,128)(2,1)S(1)}, u32[]{:S(2)}, u32[]{:S(2)}) collective-permute-start(bf16[288,128]{1,0:T(8,128)(2,1)S(1)} %get-tuple-element.96), channel_id=1, source_target_pairs={{0,8},{8,16},{16,24},{24,0},{1,9},{9,17},{17,25},{25,1},{2,10},{10... | collective-permute-start | bytes 221192 | tf_op jit(solution)/shard_map/ppermute | solution.py:314
  132.9 6.7 %collective-permute-start.11 = (bf16[288,128]{1,0:T(8,128)(2,1)S(1)}, bf16[288,128]{1,0:T(8,128)(2,1)S(1)}, u32[]{:S(2)}, u32[]{:S(2)}) collective-permute-start(bf16[288,128]{1,0:T(8,128)(2,1)S(1)} %get-tuple-element.97), channel_id=1, source_target_pairs={{0,16},{8,24},{16,0},{24,8},{1,17},{9,25},{17,1},{25,9},{2,18},{10... | collective-permute-start | bytes 221192 | tf_op jit(solution)/shard_map/ppermute | solution.py:314
  136.6 6.2 %collective-permute-start.12 = (bf16[288,128]{1,0:T(8,128)(2,1)S(1)}, bf16[288,128]{1,0:T(8,128)(2,1)S(1)}, u32[]{:S(2)}, u32[]{:S(2)}) collective-permute-start(bf16[288,128]{1,0:T(8,128)(2,1)S(1)} %get-tuple-element.98), channel_id=1, source_target_pairs={{0,24},{8,0},{16,8},{24,16},{1,25},{9,1},{17,9},{25,17},{2,26},{10... | collective-permute-start | bytes 221192 | tf_op jit(solution)/shard_map/ppermute | solution.py:314
  144.2 32.2 %copy-start.5 = (bf16[8,160,32]{2,1,0:T(8,128)(2,1)S(1)}, bf16[8,160,32]{2,1,0:T(8,128)(2,1)}, u32[]{:S(2)}) copy-start(bf16[8,160,32]{2,1,0:T(8,128)(2,1)} %copy-done.4) | copy-start | bytes 245764
  149.6 5.4 %collective-permute-start.13 = (bf16[4,4,128,128]{3,2,1,0:T(8,128)(2,1)S(1)}, bf16[4,4,128,128]{3,2,1,0:T(8,128)(2,1)S(1)}, u32[]{:S(2)}, u32[]{:S(2)}) collective-permute-start(bf16[4,4,128,128]{3,2,1,0:T(8,128)(2,1)S(1)} %get-tuple-element.100), channel_id=1, source_target_pairs={{0,1},{1,0},{2,3},{3,2},{4,5},{5,4},{6,7},{7,6},{8,9},{9,8},{10,11... | collective-permute-start | bytes 1572872 | tf_op jit(solution)/shard_map/ppermute | solution.py:314
  155.1 9.8 %collective-permute-start.14 = (bf16[4,128,128]{2,1,0:T(8,128)(2,1)S(1)}, bf16[4,128,128]{2,1,0:T(8,128)(2,1)S(1)}, u32[]{:S(2)}, u32[]{:S(2)}) collective-permute-start(bf16[4,128,128]{2,1,0:T(8,128)(2,1)S(1)} %get-tuple-element.102), channel_id=1, source_target_pairs={{0,32},{32,64},{64,96},{96,0},{1,33},{33,65},{65,97},{97,1},{2,34}... | collective-permute-start | bytes 393224 | tf_op jit(solution)/shard_map/ppermute | solution.py:314
  158.3 7.9 %collective-permute-start.15 = (bf16[4,128,128]{2,1,0:T(8,128)(2,1)S(1)}, bf16[4,128,128]{2,1,0:T(8,128)(2,1)S(1)}, u32[]{:S(2)}, u32[]{:S(2)}) collective-permute-start(bf16[4,128,128]{2,1,0:T(8,128)(2,1)S(1)} %get-tuple-element.103), channel_id=1, source_target_pairs={{0,64},{32,96},{64,0},{96,32},{1,65},{33,97},{65,1},{97,33},{2,66}... | collective-permute-start | bytes 393224 | tf_op jit(solution)/shard_map/ppermute | solution.py:314
  160.9 8.8 %collective-permute-start.16 = (bf16[4,128,128]{2,1,0:T(8,128)(2,1)S(1)}, bf16[4,128,128]{2,1,0:T(8,128)(2,1)S(1)}, u32[]{:S(2)}, u32[]{:S(2)}) collective-permute-start(bf16[4,128,128]{2,1,0:T(8,128)(2,1)S(1)} %get-tuple-element.104), channel_id=1, source_target_pairs={{0,96},{32,0},{64,32},{96,64},{1,97},{33,1},{65,33},{97,65},{2,98}... | collective-permute-start | bytes 393224 | tf_op jit(solution)/shard_map/ppermute | solution.py:314
  170.4 14.7 %all-to-all-start.5 = ((bf16[8,4,16,128]{3,2,1,0:T(8,128)(2,1)}), bf16[8,4,16,128]{3,2,1,0:T(8,128)(2,1)S(1)}, u32[]{:S(2)}, u32[]{:S(2)}) async-start(bf16[8,4,16,128]{3,2,1,0:T(8,128)(2,1)} %shard_map.129), calls=%async_computation.5 | async-start | bytes 262144 | tf_op jit(solution)/shard_map/all_to_all | solution.py:309
  178.6 78.2 %copy-start.13 = (bf16[2,32,1152]{2,1,0:T(8,128)(2,1)S(1)}, bf16[2,32,1152]{2,1,0:T(8,128)(2,1)}, u32[]{:S(2)}) copy-start(bf16[2,32,1152]{2,1,0:T(8,128)(2,1)} %get-tuple-element.80.refs_0_) | copy-start | bytes 442372
  186.0 70.9 %all-to-all-start.6 = ((bf16[4,40,1280]{2,1,0:T(8,128)(2,1)}), bf16[4,40,1280]{2,1,0:T(8,128)(2,1)S(1)}, u32[]{:S(2)}, u32[]{:S(2)}) async-start(bf16[4,40,1280]{2,1,0:T(8,128)(2,1)} %shard_map.131), calls=%async_computation.6 | async-start | bytes 819200 | tf_op jit(solution)/shard_map/all_to_all | solution.py:309
  256.9 1.5 copy-start.10
  (8 other events, 7.5 us)

commit v2 on v1

--- a/solution.py
+++ b/solution.py
@@ -221,30 +221,30 @@
     return call(route_kernel, out, at, got, jnp.asarray(table), jnp.asarray(table.T))
 
 
-def pack_kernel(level, at, picks, *refs):
+def pack_kernel(at, picks, *refs):
     held, out = refs[:-1], refs[-1]
-    total = None
-    for i, ref in enumerate(held):
-        source = (((at[0] - (i >> 1)) & 3) << 1) + ((i & 1) ^ at[1])
-        part = nn(picks[source], ref[level])
-        total = part if total is None else total + part
-    rows = out.shape[1]
-    for zh in range(ZH):
-        out[zh] = total[zh * rows : (zh + 1) * rows].astype(BF)
-
-
-def pack(at, picks, held, level):
-    out = like(ZH, picks.shape[1] // ZH, held[0].shape[-1])
-    return call(functools.partial(pack_kernel, level), out, at, picks, *held)
-
-
-def shallow_kernel(take_base, take_rest, got0, got1, rest, out_ref):
-    width = out_ref.shape[-1]
-    for level, got in enumerate((got0, got1)):
-        tap = jnp.zeros((PATCHES, width), F32)
+    rows = out.shape[2]
+    for level in range(out.shape[1]):
+        total = None
+        for i, ref in enumerate(held):
+            source = (((at[0] - (i >> 1)) & 3) << 1) + ((i & 1) ^ at[1])
+            part = nn(picks[source], ref[level])
+            total = part if total is None else total + part
         for zh in range(ZH):
-            tap += nn(take_base[zh], got[zh, :, :width])
-            tap += nn(take_rest[zh], rest[level, zh])
+            out[zh, level] = total[zh * rows : (zh + 1) * rows].astype(BF)
+
+
+def pack(at, picks, held):
+    levels, _, width = held[0].shape
+    return call(pack_kernel, like(ZH, levels, picks.shape[1] // ZH, width), at, picks, *held)
+
+
+def shallow_kernel(take_base, take_rest, got, rest, out_ref):
+    for level in range(out_ref.shape[0]):
+        tap = nn(take_base[0], got[0, level]) + nn(take_rest[0], rest[0, level])
+        for zh in range(1, ZH):
+            tap += nn(take_base[zh], got[zh, level])
+            tap += nn(take_rest[zh], rest[zh, level])
         out_ref[level] = tap.astype(BF)
 
 
@@ -275,34 +275,33 @@
         out[...] = (mine[d] + got[d].astype(F32)).astype(BF)
 
 
-def sum_y_kernel(own, g1, g2, g3, out_ref):
+def sum_y_kernel(at, own, g1, g2, g3, *outs):
+    scratch = outs[-1]
     total = own[...] + g1[...].astype(F32) + g2[...].astype(F32) + g3[...].astype(F32)
     for zl in range(ZL):
-        out_ref[zl] = total[:, zl * UPAD : (zl + 1) * UPAD, :].astype(BF)
-
-
-def join_kernel(parts, rows, out_ref):
-    width = rows.shape[-1]
-    total = parts[0].astype(F32)
-    for i in range(1, ZL):
-        total += parts[i].astype(F32)
-    out_ref[:, :, :width] = rows[...]
-    out_ref[:, :UPAD, width:] = total.astype(BF)
-    out_ref[:, UPAD:, width:] = jnp.zeros((ZH, rows.shape[1] - UPAD, 128), BF)
+        scratch[zl] = total[:, zl * UPAD : (zl + 1) * UPAD, :]
+    for d, out in enumerate(outs[:-1]):
+        out[...] = scratch[(at[4] + d) & 7].astype(out.dtype)
+
+
+def sum_zl_kernel(*refs):
+    total = refs[0][...]
+    for ref in refs[1:-1]:
+        total += ref[...].astype(F32)
+    refs[-1][...] = total.astype(BF)
 
 
 def final_kernel(factor, got, out_ref):
-    width = got.shape[-1] - 128
-    total = got[0, :UPAD, width:].astype(F32)
+    total = got[0].astype(F32)
     for i in range(1, ZH):
-        total += got[i, :UPAD, width:].astype(F32)
+        total += got[i].astype(F32)
     total = total * factor
     for g in range(GROUPS):
         out_ref[g * UNIT : (g + 1) * UNIT, :] = total[:UNIT, g * 36 : (g + 1) * 36]
 
 
-def after(x, *earlier):
-    return lax.optimization_barrier((x, *earlier))[0]
+def fence(*arrays):
+    return lax.optimization_barrier(arrays)
 
 
 def exchange(x, axes):
@@ -322,7 +321,7 @@
 def on_device(attention_out, upstream, tap_slots, owner_map, out_proj):
     width = attention_out.shape[1]
     factor = 1.0 / math.sqrt(PATCHES * ZL * Y * X * ZH * C)
-    at = jnp.stack([lax.axis_index(a) for a in ("x", "c", "zh", "y")]).astype(jnp.int32)
+    at = jnp.stack([lax.axis_index(a) for a in ("x", "c", "zh", "y", "zl")]).astype(jnp.int32)
     owners = jnp.tile(owner_map.reshape(1, M), (1, ZH)).astype(F32)
 
     q = np.arange(Y * GROUPS * ZL * UPAD)
@@ -338,15 +337,15 @@
     held2 = exchange(regroup(jnp.zeros((4,), jnp.int32), tap_slots, 2, 1, width, False), ("x", "c"))
     take2 = call(own_kernel, like(ZH, PATCHES, FULL), owners)
     got2 = exchange(call(deep_kernel, like(ZH, width // 128 * FULL + TAIL, 128), held2, owners), "zh")
-    held01 = [after(part, held2) for part in regroup(at, tap_slots, 0, 2, width, True)]
+    held01 = regroup(at, tap_slots, 0, 2, width, True)
+    held2, a_t, *held01 = fence(held2, a_t, *held01)
     held01 = [held01[0]] + [shift_xc(part, i) for i, part in enumerate(held01) if i]
-    a_t = after(a_t, held2)
     a_from = [a_t] + [shift(a_t, "x", d) for d in (1, 2, 3)]
 
-    pack_base, pack_rest, take_base, take_rest, over = route(after(at, take2, *a_from), got2)
+    got2, take2, *a_from = fence(got2, take2, *a_from)
+    pack_base, pack_rest, take_base, take_rest, over = route(at, got2)
     overflow = over[0, 0] >= BASE
-    got0 = exchange(pack(at, pack_base, held01, 0), "zh")
-    packed1 = pack(at, pack_base, held01, 1)
+    got01 = exchange(pack(at, pack_base, held01), "zh")
 
     turned = [like(width // X, PATCHES)] * X
     stream, *turned = call(
@@ -366,18 +365,20 @@
     )
     own, *parts = call(sum_c_kernel, [like(*block[1:], dtype=F32)] + [like(*block[1:])] * 3, mine, shift(other, "c", 1))
     parts = [shift(part, "y", d) for d, part in enumerate(parts, 1)]
-    partial = call(sum_y_kernel, like(ZL, ZH, UPAD, 128), own, *parts)
-    partial = exchange(after(partial, got0), "zl")
-    got1 = exchange(call(join_kernel, like(ZH, KB, width + 128), partial, packed1), "zh")
-    proj_grad = call(functools.partial(final_kernel, factor), like(36, 36, dtype=F32), got1)
+    block = (ZH, UPAD, 128)
+    scratch = [pltpu.VMEM((ZL, *block), F32)]
+    own, *parts = call(sum_y_kernel, [like(*block, dtype=F32)] + [like(*block)] * (ZL - 1), at, own, *parts, scratch=scratch)
+    parts = [shift(part, "zl", d) for d, part in enumerate(parts, 1)]
+    partial = call(sum_zl_kernel, like(*block), own, *parts)
 
     def second(picks, *held):
-        return jnp.stack([exchange(pack(at, picks, held, level), "zh") for level in (0, 1)])
-
-    rest = lax.cond(
-        overflow, second, lambda picks, *held: jnp.zeros((2, ZH, KR, width), BF), after(pack_rest, got1), *held01
-    )
-    shallow = call(shallow_kernel, like(2, PATCHES, width), take_base, take_rest, got0, got1, rest)
+        return exchange(pack(at, picks, held), "zh")
+
+    got01, pack_rest, partial = fence(got01, pack_rest, partial)
+    rest = lax.cond(overflow, second, lambda picks, *held: jnp.zeros((ZH, 2, KR, width), BF), pack_rest, *held01)
+    partial, rest = fence(partial, rest)
+    proj_grad = call(functools.partial(final_kernel, factor), like(36, 36, dtype=F32), exchange(partial, "zh"))
+    shallow = call(shallow_kernel, like(2, PATCHES, width), take_base, take_rest, got01, rest)
     return (stream, attention_grad, shallow, proj_grad)
 
 

time: 263 us -> 255 us (0.970)
  the two profiles are of different devices: /device:TPU:41 before, /device:TPU:2 now
where the time goes in v2:
time: 255 us; the launch traced here: 253 us
  starting transfers between devices  153 us (60%)
  waiting for transfers between devices  56.2 us (22%)
  Pallas kernels  23.2 us (9%)
  local copies, waits for them, and re-layouts  13.9 us (5%)
  matrix products  4.98 us (2%)
    all_to_all x4, starting transfers between devices, exchange(): return lax.all_to_all(x, axes, 0, 0, tiled=True)  72 us
    ppermute x17, starting transfers between devices, shift(): return lax.ppermute(x, axis, [(i, (i + by) % n) for i in range(n)])  59.9 us
    all_to_all x4, waiting for transfers between devices, exchange(): return lax.all_to_all(x, axes, 0, 0, tiled=True)  32.1 us
    ppermute x7, starting transfers between devices, shift_xc(): lax.ppermute(x, ('x', 'c'), [(a * C + b, (a + dx) % X * C + (b ^ dc)) for...  21.4 us
    pallas_call x11, Pallas kernels, call(): pl.pallas_call(kernel, in_specs=[smem() if a.ndim == 1 else vmem() for a...  17 us
    ppermute x17, waiting for transfers between devices, shift(): return lax.ppermute(x, axis, [(i, (i + by) % n) for i in range(n)])  13.7 us
    unnamed x48, local copies, waits for them, and re-layouts  12.7 us
    ppermute x7, waiting for transfers between devices, shift_xc(): lax.ppermute(x, ('x', 'c'), [(a * C + b, (a + dx) % X * C + (b ^ dc)) for...  10.4 us
  transfers between devices with their start and end apart: 28, of which 11 were waited for; matrix products, arithmetic and copies ran while one was open for 2% of the time, Pallas kernels for 6%

profile of v2, /device:TPU:2, one launch (start us, length us, event | category | flops | bytes accessed | tf_op | source)
XLA Modules:
  0.0 253.3 jit_solution(12631973262884912105)
XLA Ops:
  1.2 2.7 %shard_map.120 = bf16[8,1,32,1152]{3,2,1,0:T(8,128)(2,1)} custom-call(s32[4]{0:T(128)} %broadcast_3_at.2.at, bf16[3,64,4608]{2,1,0:T(8,128)(2,1)} %in_ref.3), custom_call_target="tpu_custom_call" | custom-call | tf_op jit(solution)/shard_map/pallas_call | solution.py:105
  3.9 16.8 %all-to-all-start.1 = ((bf16[8,1,32,1152]{3,2,1,0:T(8,128)(2,1)}), bf16[8,1,32,1152]{3,2,1,0:T(8,128)(2,1)S(1)}, u32[]{:S(2)}, u32[]{:S(2)}) async-start(bf16[8,1,32,1152]{3,2,1,0:T(8,128)(2,1)} %shard_map.120), calls=%async_computation.1 | async-start | bytes 1179648 | tf_op jit(solution)/shard_map/all_to_all | solution.py:308
  20.7 9.5 %all-to-all-done.1.held = bf16[8,1,32,1152]{3,2,1,0:T(8,128)(2,1)S(1)} async-done(((bf16[8,1,32,1152]{3,2,1,0:T(8,128)(2,1)}), bf16[8,1,32,1152]{3,2,1,0:T(8,128)(2,1)S(1)}, u32[]{:S(2)}, u32[]{:S(2)}) %all-to-all-start.1) | async-done | bytes 589856 | tf_op jit(solution)/shard_map/all_to_all | solution.py:308
  31.5 16.5 %all-to-all-start.2 = ((bf16[4,592,128]{2,1,0:T(8,128)(2,1)}), bf16[4,592,128]{2,1,0:T(8,128)(2,1)S(1)}, u32[]{:S(2)}, u32[]{:S(2)}) async-start(bf16[4,592,128]{2,1,0:T(8,128)(2,1)} %copy-done.2), calls=%async_computation.2 | async-start | bytes 1212416 | tf_op jit(solution)/shard_map/all_to_all | solution.py:308
  48.1 3.5 %shard_map.123 = (bf16[2,32,1152]{2,1,0:T(8,128)(2,1)}, bf16[2,32,1152]{2,1,0:T(8,128)(2,1)}, bf16[2,32,1152]{2,1,0:T(8,128)(2,1)}, bf16[2,32,1152]{2,1,0:T(8,12...) custom-call(s32[5]{0:T(128)S(1)} %stack.23.at, ...), custom_call_target="tpu_custom_call" | custom-call | tf_op jit(solution)/shard_map/pallas_call | solution.py:105
  54.0 3.4 %collective-permute-start.2 = (bf16[1536,128]{1,0:T(8,128)(2,1)S(1)}, bf16[1536,128]{1,0:T(8,128)(2,1)S(1)}, u32[]{:S(2)}, u32[]{:S(2)}) collective-permute-start(bf16[1536,128]{1,0:T(8,128)(2,1)S(1)} %fusion.2.a0), channel_id=1, source_target_pairs={{0,24},{8,0},{16,8},{24,16},{1,25},{9,1},{17,9},{25,17},{2,26},{10... | collective-permute-start | bytes 1179656 | tf_op jit(solution)/shard_map/ppermute | solution.py:313
  59.3 4.5 %collective-permute-start = (bf16[1536,128]{1,0:T(8,128)(2,1)S(1)}, bf16[1536,128]{1,0:T(8,128)(2,1)S(1)}, u32[]{:S(2)}, u32[]{:S(2)}) collective-permute-start(bf16[1536,128]{1,0:T(8,128)(2,1)S(1)} %fusion.2.a0), channel_id=1, source_target_pairs={{0,8},{8,16},{16,24},{24,0},{1,9},{9,17},{17,25},{25,1},{2,10},{10... | collective-permute-start | bytes 1179656 | tf_op jit(solution)/shard_map/ppermute | solution.py:313
  66.5 3.4 %collective-permute-start.4 = (bf16[2,32,1152]{2,1,0:T(8,128)(2,1)S(1)}, bf16[2,32,1152]{2,1,0:T(8,128)(2,1)S(1)}, u32[]{:S(2)}, u32[]{:S(2)}) collective-permute-start(bf16[2,32,1152]{2,1,0:T(8,128)(2,1)S(1)} %copy-done.20), channel_id=1, source_target_pairs={{0,8},{1,9},{8,16},{9,17},{16,24},{17,25},{24,0},{25,1},{2,10},{3,... | collective-permute-start | bytes 442376 | tf_op jit(solution)/shard_map/ppermute | solution.py:318
  69.9 2.9 %collective-permute-start.5 = (bf16[2,32,1152]{2,1,0:T(8,128)(2,1)}, bf16[2,32,1152]{2,1,0:T(8,128)(2,1)}, u32[]{:S(2)}, u32[]{:S(2)}) collective-permute-start(bf16[2,32,1152]{2,1,0:T(8,128)(2,1)} %get-tuple-element.107), channel_id=1, source_target_pairs={{0,9},{1,8},{8,17},{9,16},{16,25},{17,24},{24,1},{25,0},{2,11},{3,... | collective-permute-start | bytes 442376 | tf_op jit(solution)/shard_map/ppermute | solution.py:318
  72.8 10.4 %collective-permute-done.4.refs_2_ = bf16[2,32,1152]{2,1,0:T(8,128)(2,1)S(1)} collective-permute-done((bf16[2,32,1152]{2,1,0:T(8,128)(2,1)S(1)}, bf16[2,32,1152]{2,1,0:T(8,128)(2,1)S(1)}, u32[]{:S(2)}, u32[]{:S(2)}) %collective-permute-start.4) | collective-permute-done | bytes 147488 | tf_op jit(solution)/shard_map/ppermute | solution.py:318
  83.2 3.4 %collective-permute-start.6 = (bf16[2,32,1152]{2,1,0:T(8,128)(2,1)}, bf16[2,32,1152]{2,1,0:T(8,128)(2,1)}, u32[]{:S(2)}, u32[]{:S(2)}) collective-permute-start(bf16[2,32,1152]{2,1,0:T(8,128)(2,1)} %get-tuple-element.108), channel_id=1, source_target_pairs={{0,16},{1,17},{8,24},{9,25},{16,0},{17,1},{24,8},{25,9},{2,18},{3,... | collective-permute-start | bytes 442376 | tf_op jit(solution)/shard_map/ppermute | solution.py:318
  90.0 3.7 %collective-permute-start.8 = (bf16[2,32,1152]{2,1,0:T(8,128)(2,1)}, bf16[2,32,1152]{2,1,0:T(8,128)(2,1)}, u32[]{:S(2)}, u32[]{:S(2)}) collective-permute-start(bf16[2,32,1152]{2,1,0:T(8,128)(2,1)} %get-tuple-element.110), channel_id=1, source_target_pairs={{0,24},{1,25},{8,0},{9,1},{16,8},{17,9},{24,16},{25,17},{2,26},{3,... | collective-permute-start | bytes 442376 | tf_op jit(solution)/shard_map/ppermute | solution.py:318
  94.5 4.2 %collective-permute-start.9 = (bf16[2,32,1152]{2,1,0:T(8,128)(2,1)}, bf16[2,32,1152]{2,1,0:T(8,128)(2,1)}, u32[]{:S(2)}, u32[]{:S(2)}) collective-permute-start(bf16[2,32,1152]{2,1,0:T(8,128)(2,1)} %get-tuple-element.111), channel_id=1, source_target_pairs={{0,25},{1,24},{8,1},{9,0},{16,9},{17,8},{24,17},{25,16},{2,27},{3,... | collective-permute-start | bytes 442376 | tf_op jit(solution)/shard_map/ppermute | solution.py:318
  98.9 6.3 %all-to-all-done.2.got = bf16[4,592,128]{2,1,0:T(8,128)(2,1)S(1)} async-done(((bf16[4,592,128]{2,1,0:T(8,128)(2,1)}), bf16[4,592,128]{2,1,0:T(8,128)(2,1)S(1)}, u32[]{:S(2)}, u32[]{:S(2)}) %all-to-all-start.2) | async-done | bytes 606240 | tf_op jit(solution)/shard_map/all_to_all | solution.py:308
  108.7 3.0 %shard_map.126 = bf16[4,2,40,1152]{3,2,1,0:T(8,128)(2,1)S(1)} custom-call(s32[5]{0:T(128)S(1)} %stack.23.at, bf16[8,160,32]{2,1,0:T(8,128)(2,1)S(1)} %get-tuple-element.103.picks, bf16[2,32,1152]{2,1,0:T(8,128)(2,1)} %get-tuple-element.104.refs_0_, bf16[2,32,1152]{2,1,0:T(8,128)(2,1)} %copy-done.18, bf16[2,32,1152]{2,1,0:T(8,128)(2,1)} %copy-done.19, ...), custom_call_target="tpu_custom_call" | custom-call | tf_op jit(solution)/shard_map/pallas_call | solution.py:63
  112.6 17.1 %all-to-all-start.3 = ((bf16[4,2,40,1152]{3,2,1,0:T(8,128)(2,1)}), bf16[4,2,40,1152]{3,2,1,0:T(8,128)(2,1)}, u32[]{:S(2)}, u32[]{:S(2)}) async-start(bf16[4,2,40,1152]{3,2,1,0:T(8,128)(2,1)} %copy-done.1), calls=%async_computation.3 | async-start | bytes 1474560 | tf_op jit(solution)/shard_map/all_to_all | solution.py:308
  134.3 5.4 %collective-permute-start.11 = (bf16[288,128]{1,0:T(8,128)(2,1)S(1)}, bf16[288,128]{1,0:T(8,128)(2,1)S(1)}, u32[]{:S(2)}, u32[]{:S(2)}) collective-permute-start(bf16[288,128]{1,0:T(8,128)(2,1)S(1)} %get-tuple-element.119), channel_id=1, source_target_pairs={{0,16},{8,24},{16,0},{24,8},{1,17},{9,25},{17,1},{25,9},{2,18},{10... | collective-permute-start | bytes 221192 | tf_op jit(solution)/shard_map/ppermute | solution.py:313
  142.6 3.4 %collective-permute-done.12.s3 = bf16[288,128]{1,0:T(8,128)(2,1)S(1)} collective-permute-done((bf16[288,128]{1,0:T(8,128)(2,1)S(1)}, bf16[288,128]{1,0:T(8,128)(2,1)S(1)}, u32[]{:S(2)}, u32[]{:S(2)}) %collective-permute-start.12) | collective-permute-done | bytes 73760 | tf_op jit(solution)/shard_map/ppermute | solution.py:313
  151.4 4.5 %shard_map.127 = (f32[4,4,128,128]{3,2,1,0:T(8,128)S(1)}, bf16[4,4,128,128]{3,2,1,0:T(8,128)(2,1)S(1)}) custom-call(s32[5]{0:T(128)S(1)} %stack.23.at, bf16[1536,128]{1,0:T(8,128)(2,1)S(1)} %copy-done.5, bf16[1536,128]{1,0:T(8,128)(2,1)S(1)} %copy-done.11, bf16[1536,128]{1,0:T(8,128)(2,1)S(1)} %copy-done.9, bf16[1536,128]{1,0:T(8,128)(2,1)S(1)} %copy-done.7, ...), custom_call_target="tpu_custom_call" | custom-call | tf_op jit(solution)/shard_map/pallas_call | solution.py:63
  159.8 3.5 %collective-permute-start.14 = (bf16[4,128,128]{2,1,0:T(8,128)(2,1)S(1)}, bf16[4,128,128]{2,1,0:T(8,128)(2,1)S(1)}, u32[]{:S(2)}, u32[]{:S(2)}) collective-permute-start(bf16[4,128,128]{2,1,0:T(8,128)(2,1)S(1)} %get-tuple-element.124), channel_id=1, source_target_pairs={{0,32},{32,64},{64,96},{96,0},{1,33},{33,65},{65,97},{97,1},{2,34}... | collective-permute-start | bytes 393224 | tf_op jit(solution)/shard_map/ppermute | solution.py:313
  163.3 4.8 %collective-permute-start.15 = (bf16[4,128,128]{2,1,0:T(8,128)(2,1)S(1)}, bf16[4,128,128]{2,1,0:T(8,128)(2,1)S(1)}, u32[]{:S(2)}, u32[]{:S(2)}) collective-permute-start(bf16[4,128,128]{2,1,0:T(8,128)(2,1)S(1)} %get-tuple-element.125), channel_id=1, source_target_pairs={{0,64},{32,96},{64,0},{96,32},{1,65},{33,97},{65,1},{97,33},{2,66}... | collective-permute-start | bytes 393224 | tf_op jit(solution)/shard_map/ppermute | solution.py:313
  168.1 3.3 %collective-permute-start.16 = (bf16[4,128,128]{2,1,0:T(8,128)(2,1)S(1)}, bf16[4,128,128]{2,1,0:T(8,128)(2,1)S(1)}, u32[]{:S(2)}, u32[]{:S(2)}) collective-permute-start(bf16[4,128,128]{2,1,0:T(8,128)(2,1)S(1)} %get-tuple-element.126), channel_id=1, source_target_pairs={{0,96},{32,0},{64,32},{96,64},{1,97},{33,1},{65,33},{97,65},{2,98}... | collective-permute-start | bytes 393224 | tf_op jit(solution)/shard_map/ppermute | solution.py:313
  178.0 5.2 %collective-permute-start.18 = (bf16[4,16,128]{2,1,0:T(8,128)(2,1)S(1)}, bf16[4,16,128]{2,1,0:T(8,128)(2,1)S(1)}, u32[]{:S(2)}, u32[]{:S(2)}) collective-permute-start(bf16[4,16,128]{2,1,0:T(8,128)(2,1)S(1)} %get-tuple-element.129), channel_id=1, source_target_pairs={{0,256},{128,384},{256,512},{384,640},{512,768},{640,896},{768,0},... | collective-permute-start | bytes 49160 | tf_op jit(solution)/shard_map/ppermute | solution.py:313
  185.2 7.2 %collective-permute-start.20 = (bf16[4,16,128]{2,1,0:T(8,128)(2,1)S(1)}, bf16[4,16,128]{2,1,0:T(8,128)(2,1)S(1)}, u32[]{:S(2)}, u32[]{:S(2)}) collective-permute-start(bf16[4,16,128]{2,1,0:T(8,128)(2,1)S(1)} %get-tuple-element.131), channel_id=1, source_target_pairs={{0,512},{128,640},{256,768},{384,896},{512,0},{640,128},{768,256},... | collective-permute-start | bytes 49160 | tf_op jit(solution)/shard_map/ppermute | solution.py:313
  192.5 3.5 %collective-permute-start.21 = (bf16[4,16,128]{2,1,0:T(8,128)(2,1)S(1)}, bf16[4,16,128]{2,1,0:T(8,128)(2,1)S(1)}, u32[]{:S(2)}, u32[]{:S(2)}) collective-permute-start(bf16[4,16,128]{2,1,0:T(8,128)(2,1)S(1)} %get-tuple-element.132), channel_id=1, source_target_pairs={{0,640},{128,768},{256,896},{384,0},{512,128},{640,256},{768,384},... | collective-permute-start | bytes 49160 | tf_op jit(solution)/shard_map/ppermute | solution.py:313
  196.0 4.0 %collective-permute-done.17.refs_1_ = bf16[4,16,128]{2,1,0:T(8,128)(2,1)S(1)} collective-permute-done((bf16[4,16,128]{2,1,0:T(8,128)(2,1)S(1)}, bf16[4,16,128]{2,1,0:T(8,128)(2,1)S(1)}, u32[]{:S(2)}, u32[]{:S(2)}) %collective-permute-start.17) | collective-permute-done | bytes 16416 | tf_op jit(solution)/shard_map/ppermute | solution.py:313
  200.0 2.6 %collective-permute-start.22 = (bf16[4,16,128]{2,1,0:T(8,128)(2,1)S(1)}, bf16[4,16,128]{2,1,0:T(8,128)(2,1)S(1)}, u32[]{:S(2)}, u32[]{:S(2)}) collective-permute-start(bf16[4,16,128]{2,1,0:T(8,128)(2,1)S(1)} %get-tuple-element.133), channel_id=1, source_target_pairs={{0,768},{128,896},{256,0},{384,128},{512,256},{640,384},{768,512},... | collective-permute-start | bytes 49160 | tf_op jit(solution)/shard_map/ppermute | solution.py:313
  202.6 4.0 %collective-permute-start.23 = (bf16[4,16,128]{2,1,0:T(8,128)(2,1)S(1)}, bf16[4,16,128]{2,1,0:T(8,128)(2,1)S(1)}, u32[]{:S(2)}, u32[]{:S(2)}) collective-permute-start(bf16[4,16,128]{2,1,0:T(8,128)(2,1)S(1)} %get-tuple-element.134), channel_id=1, source_target_pairs={{0,896},{128,0},{256,128},{384,256},{512,384},{640,512},{768,640},... | collective-permute-start | bytes 49160 | tf_op jit(solution)/shard_map/ppermute | solution.py:313
  208.9 21.6 %all-to-all-start.4 = ((bf16[4,16,128]{2,1,0:T(8,128)(2,1)}), bf16[4,16,128]{2,1,0:T(8,128)(2,1)S(1)}, u32[]{:S(2)}, u32[]{:S(2)}) async-start(bf16[4,16,128]{2,1,0:T(8,128)(2,1)} %shard_map.130), calls=%async_computation.4 | async-start | bytes 32768 | tf_op jit(solution)/shard_map/all_to_all | solution.py:308
  230.5 2.6 %convolution_convert_fusion = bf16[128,1152]{1,0:T(8,128)(2,1)} fusion(bf16[128,1152]{1,0:T(8,128)(2,1)} %get-tuple-element.85, bf16[1152,1152]{1,0:T(8,128)(2,1)S(1)} %copy-done), kind=kOutput, calls=%fused_computation.4 | convolution fusion | flops 339886080 | bytes 3244032 | tf_op jit(solution)/shard_map/dot_general | solution.py:42
  233.1 3.3 %shard_map.131 = bf16[2,128,1152]{2,1,0:T(8,128)(2,1)} custom-call(bf16[4,128,40]{2,1,0:T(8,128)(2,1)S(1)} %get-tuple-element.101.take_base, bf16[4,128,24]{2,1,0:T(8,128)(2,1)S(1)} %copy-done.14, bf16[4,2,40,1152]{3,2,1,0:T(8,128)(2,1)} %all-to-all-done.3.got, bf16[4,2,24,1152]{3,2,1,0:T(8,128)(2,1)S(1)} %get-tuple-element.141.rest), custom_call_target="tpu_custom_call" | custom-call | tf_op jit(solution)/shard_map/pallas_call | solution.py:63
  236.3 16.3 %all-to-all-done.4.got = bf16[4,16,128]{2,1,0:T(8,128)(2,1)S(1)} async-done(((bf16[4,16,128]{2,1,0:T(8,128)(2,1)}), bf16[4,16,128]{2,1,0:T(8,128)(2,1)S(1)}, u32[]{:S(2)}, u32[]{:S(2)}) %all-to-all-start.4) | async-done | bytes 16416 | tf_op jit(solution)/shard_map/all_to_all | solution.py:308
  (95 shorter events, 45.4 us)
Async XLA Ops:
  0.6 229.8 %copy-start = (bf16[1152,1152]{1,0:T(8,128)(2,1)S(1)}, bf16[1152,1152]{1,0:T(8,128)(2,1)}, u32[]{:S(2)}) copy-start(bf16[1152,1152]{1,0:T(8,128)(2,1)} %param.15) | copy-start | bytes 7962628
  3.9 47.7 %copy-start.23 = (s32[1536]{0:T(1024)S(1)}, s32[1536]{0:T(1024)}, u32[]{:S(2)}) copy-start(s32[1536]{0:T(1024)} %constant.34.clone) | copy-start | bytes 18436
  3.9 26.4 %all-to-all-start.1 = ((bf16[8,1,32,1152]{3,2,1,0:T(8,128)(2,1)}), bf16[8,1,32,1152]{3,2,1,0:T(8,128)(2,1)S(1)}, u32[]{:S(2)}, u32[]{:S(2)}) async-start(bf16[8,1,32,1152]{3,2,1,0:T(8,128)(2,1)} %shard_map.120), calls=%async_computation.1 | async-start | bytes 1179648 | tf_op jit(solution)/shard_map/all_to_all | solution.py:308
  31.5 73.7 %all-to-all-start.2 = ((bf16[4,592,128]{2,1,0:T(8,128)(2,1)}), bf16[4,592,128]{2,1,0:T(8,128)(2,1)S(1)}, u32[]{:S(2)}, u32[]{:S(2)}) async-start(bf16[4,592,128]{2,1,0:T(8,128)(2,1)} %copy-done.2), calls=%async_computation.2 | async-start | bytes 1212416 | tf_op jit(solution)/shard_map/all_to_all | solution.py:308
  51.6 53.6 %copy-start.16 = (s32[8,256]{1,0:T(8,128)S(1)}, s32[8,256]{1,0:T(8,128)}, u32[]{:S(2)}) copy-start(s32[8,256]{1,0:T(8,128)} %constant.36.clone.table_ref) | copy-start | bytes 24580
  54.0 32.6 %collective-permute-start.2 = (bf16[1536,128]{1,0:T(8,128)(2,1)S(1)}, bf16[1536,128]{1,0:T(8,128)(2,1)S(1)}, u32[]{:S(2)}, u32[]{:S(2)}) collective-permute-start(bf16[1536,128]{1,0:T(8,128)(2,1)S(1)} %fusion.2.a0), channel_id=1, source_target_pairs={{0,24},{8,0},{16,8},{24,16},{1,25},{9,1},{17,9},{25,17},{2,26},{10... | collective-permute-start | bytes 1179656 | tf_op jit(solution)/shard_map/ppermute | solution.py:313
  57.3 31.9 %collective-permute-start.1 = (bf16[1536,128]{1,0:T(8,128)(2,1)S(1)}, bf16[1536,128]{1,0:T(8,128)(2,1)S(1)}, u32[]{:S(2)}, u32[]{:S(2)}) collective-permute-start(bf16[1536,128]{1,0:T(8,128)(2,1)S(1)} %fusion.2.a0), channel_id=1, source_target_pairs={{0,16},{8,24},{16,0},{24,8},{1,17},{9,25},{17,1},{25,9},{2,18},{10... | collective-permute-start | bytes 1179656 | tf_op jit(solution)/shard_map/ppermute | solution.py:313
  59.3 34.5 %collective-permute-start = (bf16[1536,128]{1,0:T(8,128)(2,1)S(1)}, bf16[1536,128]{1,0:T(8,128)(2,1)S(1)}, u32[]{:S(2)}, u32[]{:S(2)}) collective-permute-start(bf16[1536,128]{1,0:T(8,128)(2,1)S(1)} %fusion.2.a0), channel_id=1, source_target_pairs={{0,8},{8,16},{16,24},{24,0},{1,9},{9,17},{17,25},{25,1},{2,10},{10... | collective-permute-start | bytes 1179656 | tf_op jit(solution)/shard_map/ppermute | solution.py:313
  64.6 5.3 %collective-permute-start.3 = (bf16[2,32,1152]{2,1,0:T(8,128)(2,1)S(1)}, bf16[2,32,1152]{2,1,0:T(8,128)(2,1)S(1)}, u32[]{:S(2)}, u32[]{:S(2)}) collective-permute-start(bf16[2,32,1152]{2,1,0:T(8,128)(2,1)S(1)} %copy-done.21), channel_id=1, source_target_pairs={{0,1},{1,0},{8,9},{9,8},{16,17},{17,16},{24,25},{25,24},{2,3},{3,2... | collective-permute-start | bytes 442376 | tf_op jit(solution)/shard_map/ppermute | solution.py:318
  66.5 16.7 %collective-permute-start.4 = (bf16[2,32,1152]{2,1,0:T(8,128)(2,1)S(1)}, bf16[2,32,1152]{2,1,0:T(8,128)(2,1)S(1)}, u32[]{:S(2)}, u32[]{:S(2)}) collective-permute-start(bf16[2,32,1152]{2,1,0:T(8,128)(2,1)S(1)} %copy-done.20), channel_id=1, source_target_pairs={{0,8},{1,9},{8,16},{9,17},{16,24},{17,25},{24,0},{25,1},{2,10},{3,... | collective-permute-start | bytes 442376 | tf_op jit(solution)/shard_map/ppermute | solution.py:318
  69.9 38.8 %collective-permute-start.5 = (bf16[2,32,1152]{2,1,0:T(8,128)(2,1)}, bf16[2,32,1152]{2,1,0:T(8,128)(2,1)}, u32[]{:S(2)}, u32[]{:S(2)}) collective-permute-start(bf16[2,32,1152]{2,1,0:T(8,128)(2,1)} %get-tuple-element.107), channel_id=1, source_target_pairs={{0,9},{1,8},{8,17},{9,16},{16,25},{17,24},{24,1},{25,0},{2,11},{3,... | collective-permute-start | bytes 442376 | tf_op jit(solution)/shard_map/ppermute | solution.py:318
  83.2 25.5 %collective-permute-start.6 = (bf16[2,32,1152]{2,1,0:T(8,128)(2,1)}, bf16[2,32,1152]{2,1,0:T(8,128)(2,1)}, u32[]{:S(2)}, u32[]{:S(2)}) collective-permute-start(bf16[2,32,1152]{2,1,0:T(8,128)(2,1)} %get-tuple-element.108), channel_id=1, source_target_pairs={{0,16},{1,17},{8,24},{9,25},{16,0},{17,1},{24,8},{25,9},{2,18},{3,... | collective-permute-start | bytes 442376 | tf_op jit(solution)/shard_map/ppermute | solution.py:318
  87.3 21.4 %collective-permute-start.7 = (bf16[2,32,1152]{2,1,0:T(8,128)(2,1)}, bf16[2,32,1152]{2,1,0:T(8,128)(2,1)}, u32[]{:S(2)}, u32[]{:S(2)}) collective-permute-start(bf16[2,32,1152]{2,1,0:T(8,128)(2,1)} %get-tuple-element.109), channel_id=1, source_target_pairs={{0,17},{1,16},{8,25},{9,24},{16,1},{17,0},{24,9},{25,8},{2,19},{3,... | collective-permute-start | bytes 442376 | tf_op jit(solution)/shard_map/ppermute | solution.py:318
  90.0 18.7 %collective-permute-start.8 = (bf16[2,32,1152]{2,1,0:T(8,128)(2,1)}, bf16[2,32,1152]{2,1,0:T(8,128)(2,1)}, u32[]{:S(2)}, u32[]{:S(2)}) collective-permute-start(bf16[2,32,1152]{2,1,0:T(8,128)(2,1)} %get-tuple-element.110), channel_id=1, source_target_pairs={{0,24},{1,25},{8,0},{9,1},{16,8},{17,9},{24,16},{25,17},{2,26},{3,... | collective-permute-start | bytes 442376 | tf_op jit(solution)/shard_map/ppermute | solution.py:318
  94.5 14.2 %collective-permute-start.9 = (bf16[2,32,1152]{2,1,0:T(8,128)(2,1)}, bf16[2,32,1152]{2,1,0:T(8,128)(2,1)}, u32[]{:S(2)}, u32[]{:S(2)}) collective-permute-start(bf16[2,32,1152]{2,1,0:T(8,128)(2,1)} %get-tuple-element.111), channel_id=1, source_target_pairs={{0,25},{1,24},{8,1},{9,0},{16,9},{17,8},{24,17},{25,16},{2,27},{3,... | collective-permute-start | bytes 442376 | tf_op jit(solution)/shard_map/ppermute | solution.py:318
  112.6 96.3 %all-to-all-start.3 = ((bf16[4,2,40,1152]{3,2,1,0:T(8,128)(2,1)}), bf16[4,2,40,1152]{3,2,1,0:T(8,128)(2,1)}, u32[]{:S(2)}, u32[]{:S(2)}) async-start(bf16[4,2,40,1152]{3,2,1,0:T(8,128)(2,1)} %copy-done.1), calls=%async_computation.3 | async-start | bytes 1474560 | tf_op jit(solution)/shard_map/all_to_all | solution.py:308
  132.4 9.8 %collective-permute-start.10 = (bf16[288,128]{1,0:T(8,128)(2,1)S(1)}, bf16[288,128]{1,0:T(8,128)(2,1)S(1)}, u32[]{:S(2)}, u32[]{:S(2)}) collective-permute-start(bf16[288,128]{1,0:T(8,128)(2,1)S(1)} %get-tuple-element.118), channel_id=1, source_target_pairs={{0,8},{8,16},{16,24},{24,0},{1,9},{9,17},{17,25},{25,1},{2,10},{10... | collective-permute-start | bytes 221192 | tf_op jit(solution)/shard_map/ppermute | solution.py:313
  134.3 8.3 %collective-permute-start.11 = (bf16[288,128]{1,0:T(8,128)(2,1)S(1)}, bf16[288,128]{1,0:T(8,128)(2,1)S(1)}, u32[]{:S(2)}, u32[]{:S(2)}) collective-permute-start(bf16[288,128]{1,0:T(8,128)(2,1)S(1)} %get-tuple-element.119), channel_id=1, source_target_pairs={{0,16},{8,24},{16,0},{24,8},{1,17},{9,25},{17,1},{25,9},{2,18},{10... | collective-permute-start | bytes 221192 | tf_op jit(solution)/shard_map/ppermute | solution.py:313
  139.7 6.2 %collective-permute-start.12 = (bf16[288,128]{1,0:T(8,128)(2,1)S(1)}, bf16[288,128]{1,0:T(8,128)(2,1)S(1)}, u32[]{:S(2)}, u32[]{:S(2)}) collective-permute-start(bf16[288,128]{1,0:T(8,128)(2,1)S(1)} %get-tuple-element.120), channel_id=1, source_target_pairs={{0,24},{8,0},{16,8},{24,16},{1,25},{9,1},{17,9},{25,17},{2,26},{10... | collective-permute-start | bytes 221192 | tf_op jit(solution)/shard_map/ppermute | solution.py:313
  151.4 57.4 %copy-start.17 = (bf16[2,32,1152]{2,1,0:T(8,128)(2,1)S(1)}, bf16[2,32,1152]{2,1,0:T(8,128)(2,1)}, u32[]{:S(2)}) copy-start(bf16[2,32,1152]{2,1,0:T(8,128)(2,1)} %get-tuple-element.104.refs_0_) | copy-start | bytes 442372
  155.9 3.8 %collective-permute-start.13 = (bf16[4,4,128,128]{3,2,1,0:T(8,128)(2,1)S(1)}, bf16[4,4,128,128]{3,2,1,0:T(8,128)(2,1)S(1)}, u32[]{:S(2)}, u32[]{:S(2)}) collective-permute-start(bf16[4,4,128,128]{3,2,1,0:T(8,128)(2,1)S(1)} %get-tuple-element.122), channel_id=1, source_target_pairs={{0,1},{1,0},{2,3},{3,2},{4,5},{5,4},{6,7},{7,6},{8,9},{9,8},{10,11... | collective-permute-start | bytes 1572872 | tf_op jit(solution)/shard_map/ppermute | solution.py:313
  159.8 11.6 %collective-permute-start.14 = (bf16[4,128,128]{2,1,0:T(8,128)(2,1)S(1)}, bf16[4,128,128]{2,1,0:T(8,128)(2,1)S(1)}, u32[]{:S(2)}, u32[]{:S(2)}) collective-permute-start(bf16[4,128,128]{2,1,0:T(8,128)(2,1)S(1)} %get-tuple-element.124), channel_id=1, source_target_pairs={{0,32},{32,64},{64,96},{96,0},{1,33},{33,65},{65,97},{97,1},{2,34}... | collective-permute-start | bytes 393224 | tf_op jit(solution)/shard_map/ppermute | solution.py:313
  163.3 9.2 %collective-permute-start.15 = (bf16[4,128,128]{2,1,0:T(8,128)(2,1)S(1)}, bf16[4,128,128]{2,1,0:T(8,128)(2,1)S(1)}, u32[]{:S(2)}, u32[]{:S(2)}) collective-permute-start(bf16[4,128,128]{2,1,0:T(8,128)(2,1)S(1)} %get-tuple-element.125), channel_id=1, source_target_pairs={{0,64},{32,96},{64,0},{96,32},{1,65},{33,97},{65,1},{97,33},{2,66}... | collective-permute-start | bytes 393224 | tf_op jit(solution)/shard_map/ppermute | solution.py:313
  168.1 6.9 %collective-permute-start.16 = (bf16[4,128,128]{2,1,0:T(8,128)(2,1)S(1)}, bf16[4,128,128]{2,1,0:T(8,128)(2,1)S(1)}, u32[]{:S(2)}, u32[]{:S(2)}) collective-permute-start(bf16[4,128,128]{2,1,0:T(8,128)(2,1)S(1)} %get-tuple-element.126), channel_id=1, source_target_pairs={{0,96},{32,0},{64,32},{96,64},{1,97},{33,1},{65,33},{97,65},{2,98}... | collective-permute-start | bytes 393224 | tf_op jit(solution)/shard_map/ppermute | solution.py:313
  175.6 24.4 %collective-permute-start.17 = (bf16[4,16,128]{2,1,0:T(8,128)(2,1)S(1)}, bf16[4,16,128]{2,1,0:T(8,128)(2,1)S(1)}, u32[]{:S(2)}, u32[]{:S(2)}) collective-permute-start(bf16[4,16,128]{2,1,0:T(8,128)(2,1)S(1)} %get-tuple-element.128), channel_id=1, source_target_pairs={{0,128},{128,256},{256,384},{384,512},{512,640},{640,768},{768,896... | collective-permute-start | bytes 49160 | tf_op jit(solution)/shard_map/ppermute | solution.py:313
  178.0 24.5 %collective-permute-start.18 = (bf16[4,16,128]{2,1,0:T(8,128)(2,1)S(1)}, bf16[4,16,128]{2,1,0:T(8,128)(2,1)S(1)}, u32[]{:S(2)}, u32[]{:S(2)}) collective-permute-start(bf16[4,16,128]{2,1,0:T(8,128)(2,1)S(1)} %get-tuple-element.129), channel_id=1, source_target_pairs={{0,256},{128,384},{256,512},{384,640},{512,768},{640,896},{768,0},... | collective-permute-start | bytes 49160 | tf_op jit(solution)/shard_map/ppermute | solution.py:313
  183.2 24.4 %collective-permute-start.19 = (bf16[4,16,128]{2,1,0:T(8,128)(2,1)S(1)}, bf16[4,16,128]{2,1,0:T(8,128)(2,1)S(1)}, u32[]{:S(2)}, u32[]{:S(2)}) collective-permute-start(bf16[4,16,128]{2,1,0:T(8,128)(2,1)S(1)} %get-tuple-element.130), channel_id=1, source_target_pairs={{0,384},{128,512},{256,640},{384,768},{512,896},{640,0},{768,128},... | collective-permute-start | bytes 49160 | tf_op jit(solution)/shard_map/ppermute | solution.py:313
  185.2 22.4 %collective-permute-start.20 = (bf16[4,16,128]{2,1,0:T(8,128)(2,1)S(1)}, bf16[4,16,128]{2,1,0:T(8,128)(2,1)S(1)}, u32[]{:S(2)}, u32[]{:S(2)}) collective-permute-start(bf16[4,16,128]{2,1,0:T(8,128)(2,1)S(1)} %get-tuple-element.131), channel_id=1, source_target_pairs={{0,512},{128,640},{256,768},{384,896},{512,0},{640,128},{768,256},... | collective-permute-start | bytes 49160 | tf_op jit(solution)/shard_map/ppermute | solution.py:313
  192.5 15.2 %collective-permute-start.21 = (bf16[4,16,128]{2,1,0:T(8,128)(2,1)S(1)}, bf16[4,16,128]{2,1,0:T(8,128)(2,1)S(1)}, u32[]{:S(2)}, u32[]{:S(2)}) collective-permute-start(bf16[4,16,128]{2,1,0:T(8,128)(2,1)S(1)} %get-tuple-element.132), channel_id=1, source_target_pairs={{0,640},{128,768},{256,896},{384,0},{512,128},{640,256},{768,384},... | collective-permute-start | bytes 49160 | tf_op jit(solution)/shard_map/ppermute | solution.py:313
  200.0 7.7 %collective-permute-start.22 = (bf16[4,16,128]{2,1,0:T(8,128)(2,1)S(1)}, bf16[4,16,128]{2,1,0:T(8,128)(2,1)S(1)}, u32[]{:S(2)}, u32[]{:S(2)}) collective-permute-start(bf16[4,16,128]{2,1,0:T(8,128)(2,1)S(1)} %get-tuple-element.133), channel_id=1, source_target_pairs={{0,768},{128,896},{256,0},{384,128},{512,256},{640,384},{768,512},... | collective-permute-start | bytes 49160 | tf_op jit(solution)/shard_map/ppermute | solution.py:313
  202.6 5.6 %collective-permute-start.23 = (bf16[4,16,128]{2,1,0:T(8,128)(2,1)S(1)}, bf16[4,16,128]{2,1,0:T(8,128)(2,1)S(1)}, u32[]{:S(2)}, u32[]{:S(2)}) collective-permute-start(bf16[4,16,128]{2,1,0:T(8,128)(2,1)S(1)} %get-tuple-element.134), channel_id=1, source_target_pairs={{0,896},{128,0},{256,128},{384,256},{512,384},{640,512},{768,640},... | collective-permute-start | bytes 49160 | tf_op jit(solution)/shard_map/ppermute | solution.py:313
  208.9 43.8 %all-to-all-start.4 = ((bf16[4,16,128]{2,1,0:T(8,128)(2,1)}), bf16[4,16,128]{2,1,0:T(8,128)(2,1)S(1)}, u32[]{:S(2)}, u32[]{:S(2)}) async-start(bf16[4,16,128]{2,1,0:T(8,128)(2,1)} %shard_map.130), calls=%async_computation.4 | async-start | bytes 32768 | tf_op jit(solution)/shard_map/all_to_all | solution.py:308
  (20 other events, 119.3 us)

commit v3 on v2

--- a/solution.py
+++ b/solution.py
@@ -277,23 +277,19 @@
 
 def sum_y_kernel(at, own, g1, g2, g3, *outs):
     scratch = outs[-1]
+    scratch[...] = own[...] + g1[...].astype(F32) + g2[...].astype(F32) + g3[...].astype(F32)
+    for d, out in enumerate(outs[:-1]):
+        out[...] = scratch[(at[2] + d) & 3].astype(out.dtype)
+
+
+def sum_zh_kernel(own, g1, g2, g3, out_ref):
     total = own[...] + g1[...].astype(F32) + g2[...].astype(F32) + g3[...].astype(F32)
-    for zl in range(ZL):
-        scratch[zl] = total[:, zl * UPAD : (zl + 1) * UPAD, :]
-    for d, out in enumerate(outs[:-1]):
-        out[...] = scratch[(at[4] + d) & 7].astype(out.dtype)
-
-
-def sum_zl_kernel(*refs):
-    total = refs[0][...]
-    for ref in refs[1:-1]:
-        total += ref[...].astype(F32)
-    refs[-1][...] = total.astype(BF)
+    out_ref[...] = total.astype(BF).reshape(out_ref.shape)
 
 
 def final_kernel(factor, got, out_ref):
     total = got[0].astype(F32)
-    for i in range(1, ZH):
+    for i in range(1, ZL):
         total += got[i].astype(F32)
     total = total * factor
     for g in range(GROUPS):
@@ -321,7 +317,7 @@
 def on_device(attention_out, upstream, tap_slots, owner_map, out_proj):
     width = attention_out.shape[1]
     factor = 1.0 / math.sqrt(PATCHES * ZL * Y * X * ZH * C)
-    at = jnp.stack([lax.axis_index(a) for a in ("x", "c", "zh", "y", "zl")]).astype(jnp.int32)
+    at = jnp.stack([lax.axis_index(a) for a in ("x", "c", "zh", "y")]).astype(jnp.int32)
     owners = jnp.tile(owner_map.reshape(1, M), (1, ZH)).astype(F32)
 
     q = np.arange(Y * GROUPS * ZL * UPAD)
@@ -365,11 +361,11 @@
     )
     own, *parts = call(sum_c_kernel, [like(*block[1:], dtype=F32)] + [like(*block[1:])] * 3, mine, shift(other, "c", 1))
     parts = [shift(part, "y", d) for d, part in enumerate(parts, 1)]
-    block = (ZH, UPAD, 128)
-    scratch = [pltpu.VMEM((ZL, *block), F32)]
-    own, *parts = call(sum_y_kernel, [like(*block, dtype=F32)] + [like(*block)] * (ZL - 1), at, own, *parts, scratch=scratch)
-    parts = [shift(part, "zl", d) for d, part in enumerate(parts, 1)]
-    partial = call(sum_zl_kernel, like(*block), own, *parts)
+    block = (ZL * UPAD, 128)
+    scratch = [pltpu.VMEM((ZH, *block), F32)]
+    own, *parts = call(sum_y_kernel, [like(*block, dtype=F32)] + [like(*block)] * 3, at, own, *parts, scratch=scratch)
+    parts = [shift(part, "zh", d) for d, part in enumerate(parts, 1)]
+    partial = call(sum_zh_kernel, like(ZL, UPAD, 128), own, *parts)
 
     def second(picks, *held):
         return exchange(pack(at, picks, held), "zh")
@@ -377,7 +373,7 @@
     got01, pack_rest, partial = fence(got01, pack_rest, partial)
     rest = lax.cond(overflow, second, lambda picks, *held: jnp.zeros((ZH, 2, KR, width), BF), pack_rest, *held01)
     partial, rest = fence(partial, rest)
-    proj_grad = call(functools.partial(final_kernel, factor), like(36, 36, dtype=F32), exchange(partial, "zh"))
+    proj_grad = call(functools.partial(final_kernel, factor), like(36, 36, dtype=F32), exchange(partial, "zl"))
     shallow = call(shallow_kernel, like(2, PATCHES, width), take_base, take_rest, got01, rest)
     return (stream, attention_grad, shallow, proj_grad)
 

time: 255 us -> 241 us (0.945)
  the two profiles are of different devices: /device:TPU:2 before, /device:TPU:8 now
where the time goes in v3:
time: 241 us; the launch traced here: 239 us
  starting transfers between devices  145 us (60%)
  waiting for transfers between devices  50.9 us (21%)
  Pallas kernels  23.2 us (10%)
  local copies, waits for them, and re-layouts  13.8 us (6%)
  matrix products  4.98 us (2%)
    ppermute x13, starting transfers between devices, shift(): return lax.ppermute(x, axis, [(i, (i + by) % n) for i in range(n)])  66.7 us
    all_to_all x4, starting transfers between devices, exchange(): return lax.all_to_all(x, axes, 0, 0, tiled=True)  55.9 us
    all_to_all x4, waiting for transfers between devices, exchange(): return lax.all_to_all(x, axes, 0, 0, tiled=True)  23.5 us
    ppermute x7, starting transfers between devices, shift_xc(): lax.ppermute(x, ('x', 'c'), [(a * C + b, (a + dx) % X * C + (b ^ dc)) for...  22 us
    ppermute x13, waiting for transfers between devices, shift(): return lax.ppermute(x, axis, [(i, (i + by) % n) for i in range(n)])  17.4 us
    pallas_call x11, Pallas kernels, call(): pl.pallas_call(kernel, in_specs=[smem() if a.ndim == 1 else vmem() for a...  17 us
    unnamed x48, local copies, waits for them, and re-layouts  12.7 us
    ppermute x7, waiting for transfers between devices, shift_xc(): lax.ppermute(x, ('x', 'c'), [(a * C + b, (a + dx) % X * C + (b ^ dc)) for...  10.1 us
  transfers between devices with their start and end apart: 24, of which 11 were waited for; matrix products, arithmetic and copies ran while one was open for 2% of the time, Pallas kernels for 7%

profile of v3, /device:TPU:8, one launch (start us, length us, event | category | flops | bytes accessed | tf_op | source)
XLA Modules:
  0.0 239.4 jit_solution(16324070709883539426)
XLA Ops:
  1.2 2.7 %shard_map.120 = bf16[8,1,32,1152]{3,2,1,0:T(8,128)(2,1)} custom-call(s32[4]{0:T(128)} %broadcast_3_at.2.at, bf16[3,64,4608]{2,1,0:T(8,128)(2,1)} %in_ref.3), custom_call_target="tpu_custom_call" | custom-call | tf_op jit(solution)/shard_map/pallas_call | solution.py:105
  3.9 4.4 %all-to-all-start.1 = ((bf16[8,1,32,1152]{3,2,1,0:T(8,128)(2,1)}), bf16[8,1,32,1152]{3,2,1,0:T(8,128)(2,1)S(1)}, u32[]{:S(2)}, u32[]{:S(2)}) async-start(bf16[8,1,32,1152]{3,2,1,0:T(8,128)(2,1)} %shard_map.120), calls=%async_computation.1 | async-start | bytes 1179648 | tf_op jit(solution)/shard_map/all_to_all | solution.py:304
  8.4 10.9 %all-to-all-done.1.held = bf16[8,1,32,1152]{3,2,1,0:T(8,128)(2,1)S(1)} async-done(((bf16[8,1,32,1152]{3,2,1,0:T(8,128)(2,1)}), bf16[8,1,32,1152]{3,2,1,0:T(8,128)(2,1)S(1)}, u32[]{:S(2)}, u32[]{:S(2)}) %all-to-all-start.1) | async-done | bytes 589856 | tf_op jit(solution)/shard_map/all_to_all | solution.py:304
  20.6 28.3 %all-to-all-start.2 = ((bf16[4,592,128]{2,1,0:T(8,128)(2,1)}), bf16[4,592,128]{2,1,0:T(8,128)(2,1)S(1)}, u32[]{:S(2)}, u32[]{:S(2)}) async-start(bf16[4,592,128]{2,1,0:T(8,128)(2,1)} %copy-done.2), calls=%async_computation.2 | async-start | bytes 1212416 | tf_op jit(solution)/shard_map/all_to_all | solution.py:304
  49.0 3.5 %shard_map.123 = (bf16[2,32,1152]{2,1,0:T(8,128)(2,1)}, bf16[2,32,1152]{2,1,0:T(8,128)(2,1)}, bf16[2,32,1152]{2,1,0:T(8,128)(2,1)}, bf16[2,32,1152]{2,1,0:T(8,12...) custom-call(s32[4]{0:T(128)S(1)} %pad_add_fusion.at, ...), custom_call_target="tpu_custom_call" | custom-call | tf_op jit(solution)/shard_map/pallas_call | solution.py:105
  54.9 3.1 %collective-permute-start.2 = (bf16[1536,128]{1,0:T(8,128)(2,1)S(1)}, bf16[1536,128]{1,0:T(8,128)(2,1)S(1)}, u32[]{:S(2)}, u32[]{:S(2)}) collective-permute-start(bf16[1536,128]{1,0:T(8,128)(2,1)S(1)} %fusion.2.a0), channel_id=1, source_target_pairs={{0,24},{8,0},{16,8},{24,16},{1,25},{9,1},{17,9},{25,17},{2,26},{10... | collective-permute-start | bytes 1179656 | tf_op jit(solution)/shard_map/ppermute | solution.py:309
  58.0 3.4 %collective-permute-start.1 = (bf16[1536,128]{1,0:T(8,128)(2,1)S(1)}, bf16[1536,128]{1,0:T(8,128)(2,1)S(1)}, u32[]{:S(2)}, u32[]{:S(2)}) collective-permute-start(bf16[1536,128]{1,0:T(8,128)(2,1)S(1)} %fusion.2.a0), channel_id=1, source_target_pairs={{0,16},{8,24},{16,0},{24,8},{1,17},{9,25},{17,1},{25,9},{2,18},{10... | collective-permute-start | bytes 1179656 | tf_op jit(solution)/shard_map/ppermute | solution.py:309
  66.0 3.9 %collective-permute-start.4 = (bf16[2,32,1152]{2,1,0:T(8,128)(2,1)S(1)}, bf16[2,32,1152]{2,1,0:T(8,128)(2,1)S(1)}, u32[]{:S(2)}, u32[]{:S(2)}) collective-permute-start(bf16[2,32,1152]{2,1,0:T(8,128)(2,1)S(1)} %copy-done.20), channel_id=1, source_target_pairs={{0,8},{1,9},{8,16},{9,17},{16,24},{17,25},{24,0},{25,1},{2,10},{3,... | collective-permute-start | bytes 442376 | tf_op jit(solution)/shard_map/ppermute | solution.py:314
  69.9 3.2 %collective-permute-start.5 = (bf16[2,32,1152]{2,1,0:T(8,128)(2,1)}, bf16[2,32,1152]{2,1,0:T(8,128)(2,1)}, u32[]{:S(2)}, u32[]{:S(2)}) collective-permute-start(bf16[2,32,1152]{2,1,0:T(8,128)(2,1)} %get-tuple-element.103), channel_id=1, source_target_pairs={{0,9},{1,8},{8,17},{9,16},{16,25},{17,24},{24,1},{25,0},{2,11},{3,... | collective-permute-start | bytes 442376 | tf_op jit(solution)/shard_map/ppermute | solution.py:314
  73.1 10.0 %collective-permute-done.4.refs_2_ = bf16[2,32,1152]{2,1,0:T(8,128)(2,1)S(1)} collective-permute-done((bf16[2,32,1152]{2,1,0:T(8,128)(2,1)S(1)}, bf16[2,32,1152]{2,1,0:T(8,128)(2,1)S(1)}, u32[]{:S(2)}, u32[]{:S(2)}) %collective-permute-start.4) | collective-permute-done | bytes 147488 | tf_op jit(solution)/shard_map/ppermute | solution.py:314
  83.2 3.4 %collective-permute-start.6 = (bf16[2,32,1152]{2,1,0:T(8,128)(2,1)}, bf16[2,32,1152]{2,1,0:T(8,128)(2,1)}, u32[]{:S(2)}, u32[]{:S(2)}) collective-permute-start(bf16[2,32,1152]{2,1,0:T(8,128)(2,1)} %get-tuple-element.104), channel_id=1, source_target_pairs={{0,16},{1,17},{8,24},{9,25},{16,0},{17,1},{24,8},{25,9},{2,18},{3,... | collective-permute-start | bytes 442376 | tf_op jit(solution)/shard_map/ppermute | solution.py:314
  87.3 3.2 %collective-permute-start.7 = (bf16[2,32,1152]{2,1,0:T(8,128)(2,1)}, bf16[2,32,1152]{2,1,0:T(8,128)(2,1)}, u32[]{:S(2)}, u32[]{:S(2)}) collective-permute-start(bf16[2,32,1152]{2,1,0:T(8,128)(2,1)} %get-tuple-element.105), channel_id=1, source_target_pairs={{0,17},{1,16},{8,25},{9,24},{16,1},{17,0},{24,9},{25,8},{2,19},{3,... | collective-permute-start | bytes 442376 | tf_op jit(solution)/shard_map/ppermute | solution.py:314
  91.3 3.3 %collective-permute-start.8 = (bf16[2,32,1152]{2,1,0:T(8,128)(2,1)}, bf16[2,32,1152]{2,1,0:T(8,128)(2,1)}, u32[]{:S(2)}, u32[]{:S(2)}) collective-permute-start(bf16[2,32,1152]{2,1,0:T(8,128)(2,1)} %get-tuple-element.106), channel_id=1, source_target_pairs={{0,24},{1,25},{8,0},{9,1},{16,8},{17,9},{24,16},{25,17},{2,26},{3,... | collective-permute-start | bytes 442376 | tf_op jit(solution)/shard_map/ppermute | solution.py:314
  95.4 3.1 %collective-permute-start.9 = (bf16[2,32,1152]{2,1,0:T(8,128)(2,1)}, bf16[2,32,1152]{2,1,0:T(8,128)(2,1)}, u32[]{:S(2)}, u32[]{:S(2)}) collective-permute-start(bf16[2,32,1152]{2,1,0:T(8,128)(2,1)} %get-tuple-element.107), channel_id=1, source_target_pairs={{0,25},{1,24},{8,1},{9,0},{16,9},{17,8},{24,17},{25,16},{2,27},{3,... | collective-permute-start | bytes 442376 | tf_op jit(solution)/shard_map/ppermute | solution.py:314
  98.7 7.8 %all-to-all-done.2.got = bf16[4,592,128]{2,1,0:T(8,128)(2,1)S(1)} async-done(((bf16[4,592,128]{2,1,0:T(8,128)(2,1)}), bf16[4,592,128]{2,1,0:T(8,128)(2,1)S(1)}, u32[]{:S(2)}, u32[]{:S(2)}) %all-to-all-start.2) | async-done | bytes 606240 | tf_op jit(solution)/shard_map/all_to_all | solution.py:304
  109.9 3.0 %shard_map.126 = bf16[4,2,40,1152]{3,2,1,0:T(8,128)(2,1)S(1)} custom-call(s32[4]{0:T(128)S(1)} %pad_add_fusion.at, bf16[8,160,32]{2,1,0:T(8,128)(2,1)S(1)} %get-tuple-element.99.picks, bf16[2,32,1152]{2,1,0:T(8,128)(2,1)} %get-tuple-element.100.refs_0_, bf16[2,32,1152]{2,1,0:T(8,128)(2,1)} %copy-done.18, bf16[2,32,1152]{2,1,0:T(8,128)(2,1)} %copy-done.19, ...), custom_call_target="tpu_custom_call" | custom-call | tf_op jit(solution)/shard_map/pallas_call | solution.py:63
  113.8 16.8 %all-to-all-start.3 = ((bf16[4,2,40,1152]{3,2,1,0:T(8,128)(2,1)}), bf16[4,2,40,1152]{3,2,1,0:T(8,128)(2,1)}, u32[]{:S(2)}, u32[]{:S(2)}) async-start(bf16[4,2,40,1152]{3,2,1,0:T(8,128)(2,1)} %copy-done.1), calls=%async_computation.3 | async-start | bytes 1474560 | tf_op jit(solution)/shard_map/all_to_all | solution.py:304
  135.8 4.0 %collective-permute-start.11 = (bf16[288,128]{1,0:T(8,128)(2,1)S(1)}, bf16[288,128]{1,0:T(8,128)(2,1)S(1)}, u32[]{:S(2)}, u32[]{:S(2)}) collective-permute-start(bf16[288,128]{1,0:T(8,128)(2,1)S(1)} %get-tuple-element.115), channel_id=1, source_target_pairs={{0,16},{8,24},{16,0},{24,8},{1,17},{9,25},{17,1},{25,9},{2,18},{10... | collective-permute-start | bytes 221192 | tf_op jit(solution)/shard_map/ppermute | solution.py:309
  139.8 2.6 %collective-permute-start.12 = (bf16[288,128]{1,0:T(8,128)(2,1)S(1)}, bf16[288,128]{1,0:T(8,128)(2,1)S(1)}, u32[]{:S(2)}, u32[]{:S(2)}) collective-permute-start(bf16[288,128]{1,0:T(8,128)(2,1)S(1)} %get-tuple-element.116), channel_id=1, source_target_pairs={{0,24},{8,0},{16,8},{24,16},{1,25},{9,1},{17,9},{25,17},{2,26},{10... | collective-permute-start | bytes 221192 | tf_op jit(solution)/shard_map/ppermute | solution.py:309
  151.5 4.5 %shard_map.127 = (f32[4,4,128,128]{3,2,1,0:T(8,128)S(1)}, bf16[4,4,128,128]{3,2,1,0:T(8,128)(2,1)S(1)}) custom-call(s32[4]{0:T(128)S(1)} %pad_add_fusion.at, bf16[1536,128]{1,0:T(8,128)(2,1)S(1)} %copy-done.5, bf16[1536,128]{1,0:T(8,128)(2,1)S(1)} %copy-done.11, bf16[1536,128]{1,0:T(8,128)(2,1)S(1)} %copy-done.9, bf16[1536,128]{1,0:T(8,128)(2,1)S(1)} %copy-done.7, ...), custom_call_target="tpu_custom_call" | custom-call | tf_op jit(solution)/shard_map/pallas_call | solution.py:63
  159.9 3.5 %collective-permute-start.14 = (bf16[4,128,128]{2,1,0:T(8,128)(2,1)S(1)}, bf16[4,128,128]{2,1,0:T(8,128)(2,1)S(1)}, u32[]{:S(2)}, u32[]{:S(2)}) collective-permute-start(bf16[4,128,128]{2,1,0:T(8,128)(2,1)S(1)} %get-tuple-element.120), channel_id=1, source_target_pairs={{0,32},{32,64},{64,96},{96,0},{1,33},{33,65},{65,97},{97,1},{2,34}... | collective-permute-start | bytes 393224 | tf_op jit(solution)/shard_map/ppermute | solution.py:309
  163.3 2.9 %collective-permute-start.15 = (bf16[4,128,128]{2,1,0:T(8,128)(2,1)S(1)}, bf16[4,128,128]{2,1,0:T(8,128)(2,1)S(1)}, u32[]{:S(2)}, u32[]{:S(2)}) collective-permute-start(bf16[4,128,128]{2,1,0:T(8,128)(2,1)S(1)} %get-tuple-element.121), channel_id=1, source_target_pairs={{0,64},{32,96},{64,0},{96,32},{1,65},{33,97},{65,1},{97,33},{2,66}... | collective-permute-start | bytes 393224 | tf_op jit(solution)/shard_map/ppermute | solution.py:309
  166.2 4.3 %collective-permute-start.16 = (bf16[4,128,128]{2,1,0:T(8,128)(2,1)S(1)}, bf16[4,128,128]{2,1,0:T(8,128)(2,1)S(1)}, u32[]{:S(2)}, u32[]{:S(2)}) collective-permute-start(bf16[4,128,128]{2,1,0:T(8,128)(2,1)S(1)} %get-tuple-element.122), channel_id=1, source_target_pairs={{0,96},{32,0},{64,32},{96,64},{1,97},{33,1},{65,33},{97,65},{2,98}... | collective-permute-start | bytes 393224 | tf_op jit(solution)/shard_map/ppermute | solution.py:309
  175.4 12.6 %collective-permute-start.17 = (bf16[128,128]{1,0:T(8,128)(2,1)S(1)}, bf16[128,128]{1,0:T(8,128)(2,1)S(1)}, u32[]{:S(2)}, u32[]{:S(2)}) collective-permute-start(bf16[128,128]{1,0:T(8,128)(2,1)S(1)} %get-tuple-element.124), channel_id=1, source_target_pairs={{0,2},{2,4},{4,6},{6,0},{1,3},{3,5},{5,7},{7,1},{8,10},{10,12},{12... | collective-permute-start | bytes 98312 | tf_op jit(solution)/shard_map/ppermute | solution.py:309
  188.1 12.1 %collective-permute-start.18 = (bf16[128,128]{1,0:T(8,128)(2,1)S(1)}, bf16[128,128]{1,0:T(8,128)(2,1)S(1)}, u32[]{:S(2)}, u32[]{:S(2)}) collective-permute-start(bf16[128,128]{1,0:T(8,128)(2,1)S(1)} %get-tuple-element.125), channel_id=1, source_target_pairs={{0,4},{2,6},{4,0},{6,2},{1,5},{3,7},{5,1},{7,3},{8,12},{10,14},{12... | collective-permute-start | bytes 98312 | tf_op jit(solution)/shard_map/ppermute | solution.py:309
  200.2 12.1 %collective-permute-start.19 = (bf16[128,128]{1,0:T(8,128)(2,1)S(1)}, bf16[128,128]{1,0:T(8,128)(2,1)S(1)}, u32[]{:S(2)}, u32[]{:S(2)}) collective-permute-start(bf16[128,128]{1,0:T(8,128)(2,1)S(1)} %get-tuple-element.126), channel_id=1, source_target_pairs={{0,6},{2,0},{4,2},{6,4},{1,7},{3,1},{5,3},{7,5},{8,14},{10,8},{12,... | collective-permute-start | bytes 98312 | tf_op jit(solution)/shard_map/ppermute | solution.py:309
  213.5 4.5 %collective-permute-done.18.g2 = bf16[128,128]{1,0:T(8,128)(2,1)S(1)} collective-permute-done((bf16[128,128]{1,0:T(8,128)(2,1)S(1)}, bf16[128,128]{1,0:T(8,128)(2,1)S(1)}, u32[]{:S(2)}, u32[]{:S(2)}) %collective-permute-start.18) | collective-permute-done | bytes 32800 | tf_op jit(solution)/shard_map/ppermute | solution.py:309
  217.9 3.1 %collective-permute-done.19.g3 = bf16[128,128]{1,0:T(8,128)(2,1)S(1)} collective-permute-done((bf16[128,128]{1,0:T(8,128)(2,1)S(1)}, bf16[128,128]{1,0:T(8,128)(2,1)S(1)}, u32[]{:S(2)}, u32[]{:S(2)}) %collective-permute-start.19) | collective-permute-done | bytes 32800 | tf_op jit(solution)/shard_map/ppermute | solution.py:309
  221.7 6.3 %all-to-all-start.4 = ((bf16[8,16,128]{2,1,0:T(8,128)(2,1)}), bf16[8,16,128]{2,1,0:T(8,128)(2,1)S(1)}, u32[]{:S(2)}, u32[]{:S(2)}) async-start(bf16[8,16,128]{2,1,0:T(8,128)(2,1)} %shard_map.130), calls=%async_computation.4 | async-start | bytes 65536 | tf_op jit(solution)/shard_map/all_to_all | solution.py:304
  228.1 2.6 %convolution_convert_fusion = bf16[128,1152]{1,0:T(8,128)(2,1)} fusion(bf16[128,1152]{1,0:T(8,128)(2,1)} %get-tuple-element.81, bf16[1152,1152]{1,0:T(8,128)(2,1)S(1)} %copy-done), kind=kOutput, calls=%fused_computation.4 | convolution fusion | flops 339886080 | bytes 3244032 | tf_op jit(solution)/shard_map/dot_general | solution.py:42
  230.7 3.3 %shard_map.131 = bf16[2,128,1152]{2,1,0:T(8,128)(2,1)} custom-call(bf16[4,128,40]{2,1,0:T(8,128)(2,1)S(1)} %get-tuple-element.97.take_base, bf16[4,128,24]{2,1,0:T(8,128)(2,1)S(1)} %copy-done.14, bf16[4,2,40,1152]{3,2,1,0:T(8,128)(2,1)} %all-to-all-done.3.got, bf16[4,2,24,1152]{3,2,1,0:T(8,128)(2,1)S(1)} %get-tuple-element.133.rest), custom_call_target="tpu_custom_call" | custom-call | tf_op jit(solution)/shard_map/pallas_call | solution.py:63
  234.0 4.7 %all-to-all-done.4.got = bf16[8,16,128]{2,1,0:T(8,128)(2,1)S(1)} async-done(((bf16[8,16,128]{2,1,0:T(8,128)(2,1)}), bf16[8,16,128]{2,1,0:T(8,128)(2,1)S(1)}, u32[]{:S(2)}, u32[]{:S(2)}) %all-to-all-start.4) | async-done | bytes 32800 | tf_op jit(solution)/shard_map/all_to_all | solution.py:304
  (87 shorter events, 40.6 us)
Async XLA Ops:
  0.6 227.4 %copy-start = (bf16[1152,1152]{1,0:T(8,128)(2,1)S(1)}, bf16[1152,1152]{1,0:T(8,128)(2,1)}, u32[]{:S(2)}) copy-start(bf16[1152,1152]{1,0:T(8,128)(2,1)} %param.15) | copy-start | bytes 7962628
  3.9 48.6 %copy-start.23 = (s32[1536]{0:T(1024)S(1)}, s32[1536]{0:T(1024)}, u32[]{:S(2)}) copy-start(s32[1536]{0:T(1024)} %constant.30.clone) | copy-start | bytes 18436
  3.9 15.5 %all-to-all-start.1 = ((bf16[8,1,32,1152]{3,2,1,0:T(8,128)(2,1)}), bf16[8,1,32,1152]{3,2,1,0:T(8,128)(2,1)S(1)}, u32[]{:S(2)}, u32[]{:S(2)}) async-start(bf16[8,1,32,1152]{3,2,1,0:T(8,128)(2,1)} %shard_map.120), calls=%async_computation.1 | async-start | bytes 1179648 | tf_op jit(solution)/shard_map/all_to_all | solution.py:304
  20.6 85.9 %all-to-all-start.2 = ((bf16[4,592,128]{2,1,0:T(8,128)(2,1)}), bf16[4,592,128]{2,1,0:T(8,128)(2,1)S(1)}, u32[]{:S(2)}, u32[]{:S(2)}) async-start(bf16[4,592,128]{2,1,0:T(8,128)(2,1)} %copy-done.2), calls=%async_computation.2 | async-start | bytes 1212416 | tf_op jit(solution)/shard_map/all_to_all | solution.py:304
  52.5 11.6 %copy-start.21 = (bf16[2,32,1152]{2,1,0:T(8,128)(2,1)S(1)}, bf16[2,32,1152]{2,1,0:T(8,128)(2,1)}, u32[]{:S(2)}) copy-start(bf16[2,32,1152]{2,1,0:T(8,128)(2,1)} %get-tuple-element.101) | copy-start | bytes 442372
  52.5 13.5 %copy-start.20 = (bf16[2,32,1152]{2,1,0:T(8,128)(2,1)S(1)}, bf16[2,32,1152]{2,1,0:T(8,128)(2,1)}, u32[]{:S(2)}) copy-start(bf16[2,32,1152]{2,1,0:T(8,128)(2,1)} %get-tuple-element.102) | copy-start | bytes 442372
  52.5 54.0 %copy-start.16 = (s32[8,256]{1,0:T(8,128)S(1)}, s32[8,256]{1,0:T(8,128)}, u32[]{:S(2)}) copy-start(s32[8,256]{1,0:T(8,128)} %constant.32.clone.table_ref) | copy-start | bytes 24580
  54.9 31.6 %collective-permute-start.2 = (bf16[1536,128]{1,0:T(8,128)(2,1)S(1)}, bf16[1536,128]{1,0:T(8,128)(2,1)S(1)}, u32[]{:S(2)}, u32[]{:S(2)}) collective-permute-start(bf16[1536,128]{1,0:T(8,128)(2,1)S(1)} %fusion.2.a0), channel_id=1, source_target_pairs={{0,24},{8,0},{16,8},{24,16},{1,25},{9,1},{17,9},{25,17},{2,26},{10... | collective-permute-start | bytes 1179656 | tf_op jit(solution)/shard_map/ppermute | solution.py:309
  58.0 32.5 %collective-permute-start.1 = (bf16[1536,128]{1,0:T(8,128)(2,1)S(1)}, bf16[1536,128]{1,0:T(8,128)(2,1)S(1)}, u32[]{:S(2)}, u32[]{:S(2)}) collective-permute-start(bf16[1536,128]{1,0:T(8,128)(2,1)S(1)} %fusion.2.a0), channel_id=1, source_target_pairs={{0,16},{8,24},{16,0},{24,8},{1,17},{9,25},{17,1},{25,9},{2,18},{10... | collective-permute-start | bytes 1179656 | tf_op jit(solution)/shard_map/ppermute | solution.py:309
  61.4 33.2 %collective-permute-start = (bf16[1536,128]{1,0:T(8,128)(2,1)S(1)}, bf16[1536,128]{1,0:T(8,128)(2,1)S(1)}, u32[]{:S(2)}, u32[]{:S(2)}) collective-permute-start(bf16[1536,128]{1,0:T(8,128)(2,1)S(1)} %fusion.2.a0), channel_id=1, source_target_pairs={{0,8},{8,16},{16,24},{24,0},{1,9},{9,17},{17,25},{25,1},{2,10},{10... | collective-permute-start | bytes 1179656 | tf_op jit(solution)/shard_map/ppermute | solution.py:309
  64.0 5.9 %collective-permute-start.3 = (bf16[2,32,1152]{2,1,0:T(8,128)(2,1)S(1)}, bf16[2,32,1152]{2,1,0:T(8,128)(2,1)S(1)}, u32[]{:S(2)}, u32[]{:S(2)}) collective-permute-start(bf16[2,32,1152]{2,1,0:T(8,128)(2,1)S(1)} %copy-done.21), channel_id=1, source_target_pairs={{0,1},{1,0},{8,9},{9,8},{16,17},{17,16},{24,25},{25,24},{2,3},{3,2... | collective-permute-start | bytes 442376 | tf_op jit(solution)/shard_map/ppermute | solution.py:314
  66.0 17.2 %collective-permute-start.4 = (bf16[2,32,1152]{2,1,0:T(8,128)(2,1)S(1)}, bf16[2,32,1152]{2,1,0:T(8,128)(2,1)S(1)}, u32[]{:S(2)}, u32[]{:S(2)}) collective-permute-start(bf16[2,32,1152]{2,1,0:T(8,128)(2,1)S(1)} %copy-done.20), channel_id=1, source_target_pairs={{0,8},{1,9},{8,16},{9,17},{16,24},{17,25},{24,0},{25,1},{2,10},{3,... | collective-permute-start | bytes 442376 | tf_op jit(solution)/shard_map/ppermute | solution.py:314
  69.9 24.7 %copy-start.18 = (bf16[2,32,1152]{2,1,0:T(8,128)(2,1)}, bf16[2,32,1152]{2,1,0:T(8,128)(2,1)S(1)}, u32[]{:S(2)}) copy-start(bf16[2,32,1152]{2,1,0:T(8,128)(2,1)S(1)} %collective-permute-done.3.refs_1_) | copy-start | bytes 442372
  69.9 40.0 %collective-permute-start.5 = (bf16[2,32,1152]{2,1,0:T(8,128)(2,1)}, bf16[2,32,1152]{2,1,0:T(8,128)(2,1)}, u32[]{:S(2)}, u32[]{:S(2)}) collective-permute-start(bf16[2,32,1152]{2,1,0:T(8,128)(2,1)} %get-tuple-element.103), channel_id=1, source_target_pairs={{0,9},{1,8},{8,17},{9,16},{16,25},{17,24},{24,1},{25,0},{2,11},{3,... | collective-permute-start | bytes 442376 | tf_op jit(solution)/shard_map/ppermute | solution.py:314
  83.2 11.4 %copy-start.19 = (bf16[2,32,1152]{2,1,0:T(8,128)(2,1)}, bf16[2,32,1152]{2,1,0:T(8,128)(2,1)S(1)}, u32[]{:S(2)}) copy-start(bf16[2,32,1152]{2,1,0:T(8,128)(2,1)S(1)} %collective-permute-done.4.refs_2_) | copy-start | bytes 442372
  83.2 26.7 %collective-permute-start.6 = (bf16[2,32,1152]{2,1,0:T(8,128)(2,1)}, bf16[2,32,1152]{2,1,0:T(8,128)(2,1)}, u32[]{:S(2)}, u32[]{:S(2)}) collective-permute-start(bf16[2,32,1152]{2,1,0:T(8,128)(2,1)} %get-tuple-element.104), channel_id=1, source_target_pairs={{0,16},{1,17},{8,24},{9,25},{16,0},{17,1},{24,8},{25,9},{2,18},{3,... | collective-permute-start | bytes 442376 | tf_op jit(solution)/shard_map/ppermute | solution.py:314
  87.3 22.6 %collective-permute-start.7 = (bf16[2,32,1152]{2,1,0:T(8,128)(2,1)}, bf16[2,32,1152]{2,1,0:T(8,128)(2,1)}, u32[]{:S(2)}, u32[]{:S(2)}) collective-permute-start(bf16[2,32,1152]{2,1,0:T(8,128)(2,1)} %get-tuple-element.105), channel_id=1, source_target_pairs={{0,17},{1,16},{8,25},{9,24},{16,1},{17,0},{24,9},{25,8},{2,19},{3,... | collective-permute-start | bytes 442376 | tf_op jit(solution)/shard_map/ppermute | solution.py:314
  91.3 18.6 %collective-permute-start.8 = (bf16[2,32,1152]{2,1,0:T(8,128)(2,1)}, bf16[2,32,1152]{2,1,0:T(8,128)(2,1)}, u32[]{:S(2)}, u32[]{:S(2)}) collective-permute-start(bf16[2,32,1152]{2,1,0:T(8,128)(2,1)} %get-tuple-element.106), channel_id=1, source_target_pairs={{0,24},{1,25},{8,0},{9,1},{16,8},{17,9},{24,16},{25,17},{2,26},{3,... | collective-permute-start | bytes 442376 | tf_op jit(solution)/shard_map/ppermute | solution.py:314
  95.4 14.6 %collective-permute-start.9 = (bf16[2,32,1152]{2,1,0:T(8,128)(2,1)}, bf16[2,32,1152]{2,1,0:T(8,128)(2,1)}, u32[]{:S(2)}, u32[]{:S(2)}) collective-permute-start(bf16[2,32,1152]{2,1,0:T(8,128)(2,1)} %get-tuple-element.107), channel_id=1, source_target_pairs={{0,25},{1,24},{8,1},{9,0},{16,9},{17,8},{24,17},{25,16},{2,27},{3,... | collective-permute-start | bytes 442376 | tf_op jit(solution)/shard_map/ppermute | solution.py:314
  113.8 107.8 %all-to-all-start.3 = ((bf16[4,2,40,1152]{3,2,1,0:T(8,128)(2,1)}), bf16[4,2,40,1152]{3,2,1,0:T(8,128)(2,1)}, u32[]{:S(2)}, u32[]{:S(2)}) async-start(bf16[4,2,40,1152]{3,2,1,0:T(8,128)(2,1)} %copy-done.1), calls=%async_computation.3 | async-start | bytes 1474560 | tf_op jit(solution)/shard_map/all_to_all | solution.py:304
  133.3 9.0 %collective-permute-start.10 = (bf16[288,128]{1,0:T(8,128)(2,1)S(1)}, bf16[288,128]{1,0:T(8,128)(2,1)S(1)}, u32[]{:S(2)}, u32[]{:S(2)}) collective-permute-start(bf16[288,128]{1,0:T(8,128)(2,1)S(1)} %get-tuple-element.114), channel_id=1, source_target_pairs={{0,8},{8,16},{16,24},{24,0},{1,9},{9,17},{17,25},{25,1},{2,10},{10... | collective-permute-start | bytes 221192 | tf_op jit(solution)/shard_map/ppermute | solution.py:309
  135.8 7.8 %collective-permute-start.11 = (bf16[288,128]{1,0:T(8,128)(2,1)S(1)}, bf16[288,128]{1,0:T(8,128)(2,1)S(1)}, u32[]{:S(2)}, u32[]{:S(2)}) collective-permute-start(bf16[288,128]{1,0:T(8,128)(2,1)S(1)} %get-tuple-element.115), channel_id=1, source_target_pairs={{0,16},{8,24},{16,0},{24,8},{1,17},{9,25},{17,1},{25,9},{2,18},{10... | collective-permute-start | bytes 221192 | tf_op jit(solution)/shard_map/ppermute | solution.py:309
  139.8 6.2 %collective-permute-start.12 = (bf16[288,128]{1,0:T(8,128)(2,1)S(1)}, bf16[288,128]{1,0:T(8,128)(2,1)S(1)}, u32[]{:S(2)}, u32[]{:S(2)}) collective-permute-start(bf16[288,128]{1,0:T(8,128)(2,1)S(1)} %get-tuple-element.116), channel_id=1, source_target_pairs={{0,24},{8,0},{16,8},{24,16},{1,25},{9,1},{17,9},{25,17},{2,26},{10... | collective-permute-start | bytes 221192 | tf_op jit(solution)/shard_map/ppermute | solution.py:309
  151.5 70.2 %copy-start.17 = (bf16[2,32,1152]{2,1,0:T(8,128)(2,1)S(1)}, bf16[2,32,1152]{2,1,0:T(8,128)(2,1)}, u32[]{:S(2)}) copy-start(bf16[2,32,1152]{2,1,0:T(8,128)(2,1)} %get-tuple-element.100.refs_0_) | copy-start | bytes 442372
  156.0 3.8 %collective-permute-start.13 = (bf16[4,4,128,128]{3,2,1,0:T(8,128)(2,1)S(1)}, bf16[4,4,128,128]{3,2,1,0:T(8,128)(2,1)S(1)}, u32[]{:S(2)}, u32[]{:S(2)}) collective-permute-start(bf16[4,4,128,128]{3,2,1,0:T(8,128)(2,1)S(1)} %get-tuple-element.118), channel_id=1, source_target_pairs={{0,1},{1,0},{2,3},{3,2},{4,5},{5,4},{6,7},{7,6},{8,9},{9,8},{10,11... | collective-permute-start | bytes 1572872 | tf_op jit(solution)/shard_map/ppermute | solution.py:309
  159.9 10.7 %collective-permute-start.14 = (bf16[4,128,128]{2,1,0:T(8,128)(2,1)S(1)}, bf16[4,128,128]{2,1,0:T(8,128)(2,1)S(1)}, u32[]{:S(2)}, u32[]{:S(2)}) collective-permute-start(bf16[4,128,128]{2,1,0:T(8,128)(2,1)S(1)} %get-tuple-element.120), channel_id=1, source_target_pairs={{0,32},{32,64},{64,96},{96,0},{1,33},{33,65},{65,97},{97,1},{2,34}... | collective-permute-start | bytes 393224 | tf_op jit(solution)/shard_map/ppermute | solution.py:309
  163.3 9.6 %collective-permute-start.15 = (bf16[4,128,128]{2,1,0:T(8,128)(2,1)S(1)}, bf16[4,128,128]{2,1,0:T(8,128)(2,1)S(1)}, u32[]{:S(2)}, u32[]{:S(2)}) collective-permute-start(bf16[4,128,128]{2,1,0:T(8,128)(2,1)S(1)} %get-tuple-element.121), channel_id=1, source_target_pairs={{0,64},{32,96},{64,0},{96,32},{1,65},{33,97},{65,1},{97,33},{2,66}... | collective-permute-start | bytes 393224 | tf_op jit(solution)/shard_map/ppermute | solution.py:309
  166.2 8.6 %collective-permute-start.16 = (bf16[4,128,128]{2,1,0:T(8,128)(2,1)S(1)}, bf16[4,128,128]{2,1,0:T(8,128)(2,1)S(1)}, u32[]{:S(2)}, u32[]{:S(2)}) collective-permute-start(bf16[4,128,128]{2,1,0:T(8,128)(2,1)S(1)} %get-tuple-element.122), channel_id=1, source_target_pairs={{0,96},{32,0},{64,32},{96,64},{1,97},{33,1},{65,33},{97,65},{2,98}... | collective-permute-start | bytes 393224 | tf_op jit(solution)/shard_map/ppermute | solution.py:309
  175.4 38.0 %collective-permute-start.17 = (bf16[128,128]{1,0:T(8,128)(2,1)S(1)}, bf16[128,128]{1,0:T(8,128)(2,1)S(1)}, u32[]{:S(2)}, u32[]{:S(2)}) collective-permute-start(bf16[128,128]{1,0:T(8,128)(2,1)S(1)} %get-tuple-element.124), channel_id=1, source_target_pairs={{0,2},{2,4},{4,6},{6,0},{1,3},{3,5},{5,7},{7,1},{8,10},{10,12},{12... | collective-permute-start | bytes 98312 | tf_op jit(solution)/shard_map/ppermute | solution.py:309
  188.1 29.8 %collective-permute-start.18 = (bf16[128,128]{1,0:T(8,128)(2,1)S(1)}, bf16[128,128]{1,0:T(8,128)(2,1)S(1)}, u32[]{:S(2)}, u32[]{:S(2)}) collective-permute-start(bf16[128,128]{1,0:T(8,128)(2,1)S(1)} %get-tuple-element.125), channel_id=1, source_target_pairs={{0,4},{2,6},{4,0},{6,2},{1,5},{3,7},{5,1},{7,3},{8,12},{10,14},{12... | collective-permute-start | bytes 98312 | tf_op jit(solution)/shard_map/ppermute | solution.py:309
  200.2 20.9 %collective-permute-start.19 = (bf16[128,128]{1,0:T(8,128)(2,1)S(1)}, bf16[128,128]{1,0:T(8,128)(2,1)S(1)}, u32[]{:S(2)}, u32[]{:S(2)}) collective-permute-start(bf16[128,128]{1,0:T(8,128)(2,1)S(1)} %get-tuple-element.126), channel_id=1, source_target_pairs={{0,6},{2,0},{4,2},{6,4},{1,7},{3,1},{5,3},{7,5},{8,14},{10,8},{12,... | collective-permute-start | bytes 98312 | tf_op jit(solution)/shard_map/ppermute | solution.py:309
  221.7 17.0 %all-to-all-start.4 = ((bf16[8,16,128]{2,1,0:T(8,128)(2,1)}), bf16[8,16,128]{2,1,0:T(8,128)(2,1)S(1)}, u32[]{:S(2)}, u32[]{:S(2)}) async-start(bf16[8,16,128]{2,1,0:T(8,128)(2,1)} %shard_map.130), calls=%async_computation.4 | async-start | bytes 65536 | tf_op jit(solution)/shard_map/all_to_all | solution.py:304
  (16 other events, 29.4 us)

commit v4 on v3

--- a/solution.py
+++ b/solution.py
@@ -275,16 +275,20 @@
         out[...] = (mine[d] + got[d].astype(F32)).astype(BF)
 
 
-def sum_y_kernel(at, own, g1, g2, g3, *outs):
-    scratch = outs[-1]
+def sum_y_kernel(at, own, g1, g2, g3, keep, send, scratch):
     scratch[...] = own[...] + g1[...].astype(F32) + g2[...].astype(F32) + g3[...].astype(F32)
-    for d, out in enumerate(outs[:-1]):
-        out[...] = scratch[(at[2] + d) & 3].astype(out.dtype)
-
-
-def sum_zh_kernel(own, g1, g2, g3, out_ref):
-    total = own[...] + g1[...].astype(F32) + g2[...].astype(F32) + g3[...].astype(F32)
-    out_ref[...] = total.astype(BF).reshape(out_ref.shape)
+    for d in range(2):
+        keep[d] = scratch[at[2] ^ d]
+        send[d] = scratch[at[2] ^ 2 ^ d].astype(BF)
+
+
+def sum_far_kernel(keep, got, mine, send):
+    mine[...] = keep[0] + got[0].astype(F32)
+    send[...] = keep[1] + got[1].astype(F32)
+
+
+def sum_near_kernel(mine, got, out_ref):
+    out_ref[...] = (mine[...] + got[...]).astype(BF).reshape(out_ref.shape)
 
 
 def final_kernel(factor, got, out_ref):
@@ -307,6 +311,10 @@
 def shift(x, axis, by):
     n = lax.axis_size(axis)
     return lax.ppermute(x, axis, [(i, (i + by) % n) for i in range(n)])
+
+
+def swap(x, bit):
+    return lax.ppermute(x, "zh", [(i, i ^ bit) for i in range(ZH)])
 
 
 def shift_xc(x, i):
@@ -363,9 +371,10 @@
     parts = [shift(part, "y", d) for d, part in enumerate(parts, 1)]
     block = (ZL * UPAD, 128)
     scratch = [pltpu.VMEM((ZH, *block), F32)]
-    own, *parts = call(sum_y_kernel, [like(*block, dtype=F32)] + [like(*block)] * 3, at, own, *parts, scratch=scratch)
-    parts = [shift(part, "zh", d) for d, part in enumerate(parts, 1)]
-    partial = call(sum_zh_kernel, like(ZL, UPAD, 128), own, *parts)
+    out = [like(2, *block, dtype=F32), like(2, *block)]
+    keep, send = call(sum_y_kernel, out, at, own, *parts, scratch=scratch)
+    own, send = call(sum_far_kernel, [like(*block, dtype=F32)] * 2, keep, swap(send, 2))
+    partial = call(sum_near_kernel, like(ZL, UPAD, 128), own, swap(send, 1))
 
     def second(picks, *held):
         return exchange(pack(at, picks, held), "zh")

time: 241 us -> 259 us (1.075)
  the two profiles are of different devices: /device:TPU:8 before, /device:TPU:26 now
where the time goes in v4:
time: 259 us; the launch traced here: 258 us
  starting transfers between devices  143 us (55%)
  waiting for transfers between devices  71.6 us (28%)
  Pallas kernels  23.2 us (9%)
  local copies, waits for them, and re-layouts  13.8 us (5%)
  matrix products  4.98 us (2%)
    all_to_all x4, starting transfers between devices, exchange(): return lax.all_to_all(x, axes, 0, 0, tiled=True)  53.5 us
    ppermute x2, starting transfers between devices, swap(): return lax.ppermute(x, 'zh', [(i, i ^ bit) for i in range(ZH)])  37.6 us
    ppermute x10, starting transfers between devices, shift(): return lax.ppermute(x, axis, [(i, (i + by) % n) for i in range(n)])  30.1 us
    ppermute x2, waiting for transfers between devices, swap(): return lax.ppermute(x, 'zh', [(i, i ^ bit) for i in range(ZH)])  28.7 us
    ppermute x7, starting transfers between devices, shift_xc(): lax.ppermute(x, ('x', 'c'), [(a * C + b, (a + dx) % X * C + (b ^ dc)) for...  21.4 us
    all_to_all x4, waiting for transfers between devices, exchange(): return lax.all_to_all(x, axes, 0, 0, tiled=True)  20.7 us
    pallas_call x12, Pallas kernels, call(): pl.pallas_call(kernel, in_specs=[smem() if a.ndim == 1 else vmem() for a...  17 us
    unnamed x48, local copies, waits for them, and re-layouts  12.7 us
  transfers between devices with their start and end apart: 23, of which 11 were waited for; matrix products, arithmetic and copies ran while one was open for 2% of the time, Pallas kernels for 6%

profile of v4, /device:TPU:26, one launch (start us, length us, event | category | flops | bytes accessed | tf_op | source)
XLA Modules:
  0.0 258.0 jit_solution(9996499535516977212)
XLA Ops:
  1.2 2.7 %shard_map.120 = bf16[8,1,32,1152]{3,2,1,0:T(8,128)(2,1)} custom-call(s32[4]{0:T(128)} %broadcast_3_at.2.at, bf16[3,64,4608]{2,1,0:T(8,128)(2,1)} %in_ref.3), custom_call_target="tpu_custom_call" | custom-call | tf_op jit(solution)/shard_map/pallas_call | solution.py:105
  3.9 5.0 %all-to-all-start.1 = ((bf16[8,1,32,1152]{3,2,1,0:T(8,128)(2,1)}), bf16[8,1,32,1152]{3,2,1,0:T(8,128)(2,1)S(1)}, u32[]{:S(2)}, u32[]{:S(2)}) async-start(bf16[8,1,32,1152]{3,2,1,0:T(8,128)(2,1)} %shard_map.120), calls=%async_computation.1 | async-start | bytes 1179648 | tf_op jit(solution)/shard_map/all_to_all | solution.py:308
  8.9 9.5 %all-to-all-done.1.held = bf16[8,1,32,1152]{3,2,1,0:T(8,128)(2,1)S(1)} async-done(((bf16[8,1,32,1152]{3,2,1,0:T(8,128)(2,1)}), bf16[8,1,32,1152]{3,2,1,0:T(8,128)(2,1)S(1)}, u32[]{:S(2)}, u32[]{:S(2)}) %all-to-all-start.1) | async-done | bytes 589856 | tf_op jit(solution)/shard_map/all_to_all | solution.py:308
  19.6 28.3 %all-to-all-start.2 = ((bf16[4,592,128]{2,1,0:T(8,128)(2,1)}), bf16[4,592,128]{2,1,0:T(8,128)(2,1)S(1)}, u32[]{:S(2)}, u32[]{:S(2)}) async-start(bf16[4,592,128]{2,1,0:T(8,128)(2,1)} %copy-done.2), calls=%async_computation.2 | async-start | bytes 1212416 | tf_op jit(solution)/shard_map/all_to_all | solution.py:308
  48.1 3.5 %shard_map.123 = (bf16[2,32,1152]{2,1,0:T(8,128)(2,1)}, bf16[2,32,1152]{2,1,0:T(8,128)(2,1)}, bf16[2,32,1152]{2,1,0:T(8,128)(2,1)}, bf16[2,32,1152]{2,1,0:T(8,12...) custom-call(s32[4]{0:T(128)S(1)} %pad_add_fusion.at, ...), custom_call_target="tpu_custom_call" | custom-call | tf_op jit(solution)/shard_map/pallas_call | solution.py:105
  51.6 2.4 fusion.2.a0
  54.0 3.4 %collective-permute-start.2 = (bf16[1536,128]{1,0:T(8,128)(2,1)S(1)}, bf16[1536,128]{1,0:T(8,128)(2,1)S(1)}, u32[]{:S(2)}, u32[]{:S(2)}) collective-permute-start(bf16[1536,128]{1,0:T(8,128)(2,1)S(1)} %fusion.2.a0), channel_id=1, source_target_pairs={{0,24},{8,0},{16,8},{24,16},{1,25},{9,1},{17,9},{25,17},{2,26},{10... | collective-permute-start | bytes 1179656 | tf_op jit(solution)/shard_map/ppermute | solution.py:313
  59.3 4.5 %collective-permute-start = (bf16[1536,128]{1,0:T(8,128)(2,1)S(1)}, bf16[1536,128]{1,0:T(8,128)(2,1)S(1)}, u32[]{:S(2)}, u32[]{:S(2)}) collective-permute-start(bf16[1536,128]{1,0:T(8,128)(2,1)S(1)} %fusion.2.a0), channel_id=1, source_target_pairs={{0,8},{8,16},{16,24},{24,0},{1,9},{9,17},{17,25},{25,1},{2,10},{10... | collective-permute-start | bytes 1179656 | tf_op jit(solution)/shard_map/ppermute | solution.py:313
  66.5 3.4 %collective-permute-start.4 = (bf16[2,32,1152]{2,1,0:T(8,128)(2,1)S(1)}, bf16[2,32,1152]{2,1,0:T(8,128)(2,1)S(1)}, u32[]{:S(2)}, u32[]{:S(2)}) collective-permute-start(bf16[2,32,1152]{2,1,0:T(8,128)(2,1)S(1)} %copy-done.20), channel_id=1, source_target_pairs={{0,8},{1,9},{8,16},{9,17},{16,24},{17,25},{24,0},{25,1},{2,10},{3,... | collective-permute-start | bytes 442376 | tf_op jit(solution)/shard_map/ppermute | solution.py:322
  69.9 2.9 %collective-permute-start.5 = (bf16[2,32,1152]{2,1,0:T(8,128)(2,1)}, bf16[2,32,1152]{2,1,0:T(8,128)(2,1)}, u32[]{:S(2)}, u32[]{:S(2)}) collective-permute-start(bf16[2,32,1152]{2,1,0:T(8,128)(2,1)} %get-tuple-element.103), channel_id=1, source_target_pairs={{0,9},{1,8},{8,17},{9,16},{16,25},{17,24},{24,1},{25,0},{2,11},{3,... | collective-permute-start | bytes 442376 | tf_op jit(solution)/shard_map/ppermute | solution.py:322
  72.8 10.4 %collective-permute-done.4.refs_2_ = bf16[2,32,1152]{2,1,0:T(8,128)(2,1)S(1)} collective-permute-done((bf16[2,32,1152]{2,1,0:T(8,128)(2,1)S(1)}, bf16[2,32,1152]{2,1,0:T(8,128)(2,1)S(1)}, u32[]{:S(2)}, u32[]{:S(2)}) %collective-permute-start.4) | collective-permute-done | bytes 147488 | tf_op jit(solution)/shard_map/ppermute | solution.py:322
  83.2 3.4 %collective-permute-start.6 = (bf16[2,32,1152]{2,1,0:T(8,128)(2,1)}, bf16[2,32,1152]{2,1,0:T(8,128)(2,1)}, u32[]{:S(2)}, u32[]{:S(2)}) collective-permute-start(bf16[2,32,1152]{2,1,0:T(8,128)(2,1)} %get-tuple-element.104), channel_id=1, source_target_pairs={{0,16},{1,17},{8,24},{9,25},{16,0},{17,1},{24,8},{25,9},{2,18},{3,... | collective-permute-start | bytes 442376 | tf_op jit(solution)/shard_map/ppermute | solution.py:322
  90.0 3.7 %collective-permute-start.8 = (bf16[2,32,1152]{2,1,0:T(8,128)(2,1)}, bf16[2,32,1152]{2,1,0:T(8,128)(2,1)}, u32[]{:S(2)}, u32[]{:S(2)}) collective-permute-start(bf16[2,32,1152]{2,1,0:T(8,128)(2,1)} %get-tuple-element.106), channel_id=1, source_target_pairs={{0,24},{1,25},{8,0},{9,1},{16,8},{17,9},{24,16},{25,17},{2,26},{3,... | collective-permute-start | bytes 442376 | tf_op jit(solution)/shard_map/ppermute | solution.py:322
  94.5 4.2 %collective-permute-start.9 = (bf16[2,32,1152]{2,1,0:T(8,128)(2,1)}, bf16[2,32,1152]{2,1,0:T(8,128)(2,1)}, u32[]{:S(2)}, u32[]{:S(2)}) collective-permute-start(bf16[2,32,1152]{2,1,0:T(8,128)(2,1)} %get-tuple-element.107), channel_id=1, source_target_pairs={{0,25},{1,24},{8,1},{9,0},{16,9},{17,8},{24,17},{25,16},{2,27},{3,... | collective-permute-start | bytes 442376 | tf_op jit(solution)/shard_map/ppermute | solution.py:322
  98.9 6.5 %all-to-all-done.2.got = bf16[4,592,128]{2,1,0:T(8,128)(2,1)S(1)} async-done(((bf16[4,592,128]{2,1,0:T(8,128)(2,1)}), bf16[4,592,128]{2,1,0:T(8,128)(2,1)S(1)}, u32[]{:S(2)}, u32[]{:S(2)}) %all-to-all-start.2) | async-done | bytes 606240 | tf_op jit(solution)/shard_map/all_to_all | solution.py:308
  108.9 3.0 %shard_map.126 = bf16[4,2,40,1152]{3,2,1,0:T(8,128)(2,1)S(1)} custom-call(s32[4]{0:T(128)S(1)} %pad_add_fusion.at, bf16[8,160,32]{2,1,0:T(8,128)(2,1)S(1)} %get-tuple-element.99.picks, bf16[2,32,1152]{2,1,0:T(8,128)(2,1)} %get-tuple-element.100.refs_0_, bf16[2,32,1152]{2,1,0:T(8,128)(2,1)} %copy-done.18, bf16[2,32,1152]{2,1,0:T(8,128)(2,1)} %copy-done.19, ...), custom_call_target="tpu_custom_call" | custom-call | tf_op jit(solution)/shard_map/pallas_call | solution.py:63
  112.8 16.9 %all-to-all-start.3 = ((bf16[4,2,40,1152]{3,2,1,0:T(8,128)(2,1)}), bf16[4,2,40,1152]{3,2,1,0:T(8,128)(2,1)}, u32[]{:S(2)}, u32[]{:S(2)}) async-start(bf16[4,2,40,1152]{3,2,1,0:T(8,128)(2,1)} %copy-done.1), calls=%async_computation.3 | async-start | bytes 1474560 | tf_op jit(solution)/shard_map/all_to_all | solution.py:308
  134.3 5.4 %collective-permute-start.11 = (bf16[288,128]{1,0:T(8,128)(2,1)S(1)}, bf16[288,128]{1,0:T(8,128)(2,1)S(1)}, u32[]{:S(2)}, u32[]{:S(2)}) collective-permute-start(bf16[288,128]{1,0:T(8,128)(2,1)S(1)} %get-tuple-element.115), channel_id=1, source_target_pairs={{0,16},{8,24},{16,0},{24,8},{1,17},{9,25},{17,1},{25,9},{2,18},{10... | collective-permute-start | bytes 221192 | tf_op jit(solution)/shard_map/ppermute | solution.py:313
  139.7 2.5 collective-permute-start.12
  142.6 3.4 %collective-permute-done.12.s3 = bf16[288,128]{1,0:T(8,128)(2,1)S(1)} collective-permute-done((bf16[288,128]{1,0:T(8,128)(2,1)S(1)}, bf16[288,128]{1,0:T(8,128)(2,1)S(1)}, u32[]{:S(2)}, u32[]{:S(2)}) %collective-permute-start.12) | collective-permute-done | bytes 73760 | tf_op jit(solution)/shard_map/ppermute | solution.py:313
  151.5 4.5 %shard_map.127 = (f32[4,4,128,128]{3,2,1,0:T(8,128)S(1)}, bf16[4,4,128,128]{3,2,1,0:T(8,128)(2,1)S(1)}) custom-call(s32[4]{0:T(128)S(1)} %pad_add_fusion.at, bf16[1536,128]{1,0:T(8,128)(2,1)S(1)} %copy-done.5, bf16[1536,128]{1,0:T(8,128)(2,1)S(1)} %copy-done.11, bf16[1536,128]{1,0:T(8,128)(2,1)S(1)} %copy-done.9, bf16[1536,128]{1,0:T(8,128)(2,1)S(1)} %copy-done.7, ...), custom_call_target="tpu_custom_call" | custom-call | tf_op jit(solution)/shard_map/pallas_call | solution.py:63
  162.0 4.5 %collective-permute-start.15 = (bf16[4,128,128]{2,1,0:T(8,128)(2,1)S(1)}, bf16[4,128,128]{2,1,0:T(8,128)(2,1)S(1)}, u32[]{:S(2)}, u32[]{:S(2)}) collective-permute-start(bf16[4,128,128]{2,1,0:T(8,128)(2,1)S(1)} %get-tuple-element.121), channel_id=1, source_target_pairs={{0,64},{32,96},{64,0},{96,32},{1,65},{33,97},{65,1},{97,33},{2,66}... | collective-permute-start | bytes 393224 | tf_op jit(solution)/shard_map/ppermute | solution.py:313
  168.4 2.3 collective-permute-done.15.g2
  170.7 3.9 %collective-permute-done.16.g3 = bf16[4,128,128]{2,1,0:T(8,128)(2,1)S(1)} collective-permute-done((bf16[4,128,128]{2,1,0:T(8,128)(2,1)S(1)}, bf16[4,128,128]{2,1,0:T(8,128)(2,1)S(1)}, u32[]{:S(2)}, u32[]{:S(2)}) %collective-permute-start.16) | collective-permute-done | bytes 131104 | tf_op jit(solution)/shard_map/ppermute | solution.py:313
  175.2 22.2 %collective-permute-start.17 = (bf16[2,128,128]{2,1,0:T(8,128)(2,1)S(1)}, bf16[2,128,128]{2,1,0:T(8,128)(2,1)S(1)}, u32[]{:S(2)}, u32[]{:S(2)}) collective-permute-start(bf16[2,128,128]{2,1,0:T(8,128)(2,1)S(1)} %get-tuple-element.124), channel_id=1, source_target_pairs={{0,4},{2,6},{4,0},{6,2},{1,5},{3,7},{5,1},{7,3},{8,12},{10,14},{12... | collective-permute-start | bytes 196616 | tf_op jit(solution)/shard_map/ppermute | solution.py:317
  197.4 18.3 %collective-permute-done.17.got = bf16[2,128,128]{2,1,0:T(8,128)(2,1)S(1)} collective-permute-done((bf16[2,128,128]{2,1,0:T(8,128)(2,1)S(1)}, bf16[2,128,128]{2,1,0:T(8,128)(2,1)S(1)}, u32[]{:S(2)}, u32[]{:S(2)}) %collective-permute-start.17) | collective-permute-done | bytes 65568 | tf_op jit(solution)/shard_map/ppermute | solution.py:317
  215.8 15.3 %collective-permute-start.18 = (f32[128,128]{1,0:T(8,128)S(1)}, f32[128,128]{1,0:T(8,128)S(1)}, u32[]{:S(2)}, u32[]{:S(2)}) collective-permute-start(f32[128,128]{1,0:T(8,128)S(1)} %get-tuple-element.126), channel_id=1, source_target_pairs={{0,2},{2,0},{4,6},{6,4},{1,3},{3,1},{5,7},{7,5},{8,10},{10,8},{12,... | collective-permute-start | bytes 196616 | tf_op jit(solution)/shard_map/ppermute | solution.py:317
  232.3 10.4 %collective-permute-done.18.got = f32[128,128]{1,0:T(8,128)S(1)} collective-permute-done((f32[128,128]{1,0:T(8,128)S(1)}, f32[128,128]{1,0:T(8,128)S(1)}, u32[]{:S(2)}, u32[]{:S(2)}) %collective-permute-start.18) | collective-permute-done | bytes 65568 | tf_op jit(solution)/shard_map/ppermute | solution.py:317
  243.4 3.3 %all-to-all-start.4 = ((bf16[8,16,128]{2,1,0:T(8,128)(2,1)}), bf16[8,16,128]{2,1,0:T(8,128)(2,1)S(1)}, u32[]{:S(2)}, u32[]{:S(2)}) async-start(bf16[8,16,128]{2,1,0:T(8,128)(2,1)} %shard_map.131), calls=%async_computation.4 | async-start | bytes 65536 | tf_op jit(solution)/shard_map/all_to_all | solution.py:308
  246.8 2.6 %convolution_convert_fusion = bf16[128,1152]{1,0:T(8,128)(2,1)} fusion(bf16[128,1152]{1,0:T(8,128)(2,1)} %get-tuple-element.81, bf16[1152,1152]{1,0:T(8,128)(2,1)S(1)} %copy-done), kind=kOutput, calls=%fused_computation.4 | convolution fusion | flops 339886080 | bytes 3244032 | tf_op jit(solution)/shard_map/dot_general | solution.py:42
  249.3 3.3 %shard_map.132 = bf16[2,128,1152]{2,1,0:T(8,128)(2,1)} custom-call(bf16[4,128,40]{2,1,0:T(8,128)(2,1)S(1)} %get-tuple-element.97.take_base, bf16[4,128,24]{2,1,0:T(8,128)(2,1)S(1)} %copy-done.14, bf16[4,2,40,1152]{3,2,1,0:T(8,128)(2,1)} %all-to-all-done.3.got, bf16[4,2,24,1152]{3,2,1,0:T(8,128)(2,1)S(1)} %get-tuple-element.133.rest), custom_call_target="tpu_custom_call" | custom-call | tf_op jit(solution)/shard_map/pallas_call | solution.py:63
  252.6 4.7 %all-to-all-done.4.got = bf16[8,16,128]{2,1,0:T(8,128)(2,1)S(1)} async-done(((bf16[8,16,128]{2,1,0:T(8,128)(2,1)}), bf16[8,16,128]{2,1,0:T(8,128)(2,1)S(1)}, u32[]{:S(2)}, u32[]{:S(2)}) %all-to-all-start.4) | async-done | bytes 32800 | tf_op jit(solution)/shard_map/all_to_all | solution.py:308
  (86 shorter events, 36.2 us)
Async XLA Ops:
  0.6 246.1 %copy-start = (bf16[1152,1152]{1,0:T(8,128)(2,1)S(1)}, bf16[1152,1152]{1,0:T(8,128)(2,1)}, u32[]{:S(2)}) copy-start(bf16[1152,1152]{1,0:T(8,128)(2,1)} %param.15) | copy-start | bytes 7962628
  0.6 8.2 %copy-start.22 = (s32[32,1]{0,1:T(1,128)S(1)}, s32[32,1]{0,1:T(1,128)}, u32[]{:S(2)}) copy-start(s32[32,1]{0,1:T(1,128)} %param.14) | copy-start | bytes 388
  3.9 47.7 %copy-start.23 = (s32[1536]{0:T(1024)S(1)}, s32[1536]{0:T(1024)}, u32[]{:S(2)}) copy-start(s32[1536]{0:T(1024)} %constant.30.clone) | copy-start | bytes 18436
  3.9 14.6 %all-to-all-start.1 = ((bf16[8,1,32,1152]{3,2,1,0:T(8,128)(2,1)}), bf16[8,1,32,1152]{3,2,1,0:T(8,128)(2,1)S(1)}, u32[]{:S(2)}, u32[]{:S(2)}) async-start(bf16[8,1,32,1152]{3,2,1,0:T(8,128)(2,1)} %shard_map.120), calls=%async_computation.1 | async-start | bytes 1179648 | tf_op jit(solution)/shard_map/all_to_all | solution.py:308
  19.6 85.8 %all-to-all-start.2 = ((bf16[4,592,128]{2,1,0:T(8,128)(2,1)}), bf16[4,592,128]{2,1,0:T(8,128)(2,1)S(1)}, u32[]{:S(2)}, u32[]{:S(2)}) async-start(bf16[4,592,128]{2,1,0:T(8,128)(2,1)} %copy-done.2), calls=%async_computation.2 | async-start | bytes 1212416 | tf_op jit(solution)/shard_map/all_to_all | solution.py:308
  51.5 13.0 %copy-start.21 = (bf16[2,32,1152]{2,1,0:T(8,128)(2,1)S(1)}, bf16[2,32,1152]{2,1,0:T(8,128)(2,1)}, u32[]{:S(2)}) copy-start(bf16[2,32,1152]{2,1,0:T(8,128)(2,1)} %get-tuple-element.101) | copy-start | bytes 442372
  51.5 14.9 %copy-start.20 = (bf16[2,32,1152]{2,1,0:T(8,128)(2,1)S(1)}, bf16[2,32,1152]{2,1,0:T(8,128)(2,1)}, u32[]{:S(2)}) copy-start(bf16[2,32,1152]{2,1,0:T(8,128)(2,1)} %get-tuple-element.102) | copy-start | bytes 442372
  51.6 53.9 %copy-start.16 = (s32[8,256]{1,0:T(8,128)S(1)}, s32[8,256]{1,0:T(8,128)}, u32[]{:S(2)}) copy-start(s32[8,256]{1,0:T(8,128)} %constant.32.clone.table_ref) | copy-start | bytes 24580
  54.0 32.6 %collective-permute-start.2 = (bf16[1536,128]{1,0:T(8,128)(2,1)S(1)}, bf16[1536,128]{1,0:T(8,128)(2,1)S(1)}, u32[]{:S(2)}, u32[]{:S(2)}) collective-permute-start(bf16[1536,128]{1,0:T(8,128)(2,1)S(1)} %fusion.2.a0), channel_id=1, source_target_pairs={{0,24},{8,0},{16,8},{24,16},{1,25},{9,1},{17,9},{25,17},{2,26},{10... | collective-permute-start | bytes 1179656 | tf_op jit(solution)/shard_map/ppermute | solution.py:313
  57.4 31.8 %collective-permute-start.1 = (bf16[1536,128]{1,0:T(8,128)(2,1)S(1)}, bf16[1536,128]{1,0:T(8,128)(2,1)S(1)}, u32[]{:S(2)}, u32[]{:S(2)}) collective-permute-start(bf16[1536,128]{1,0:T(8,128)(2,1)S(1)} %fusion.2.a0), channel_id=1, source_target_pairs={{0,16},{8,24},{16,0},{24,8},{1,17},{9,25},{17,1},{25,9},{2,18},{10... | collective-permute-start | bytes 1179656 | tf_op jit(solution)/shard_map/ppermute | solution.py:313
  59.3 34.4 %collective-permute-start = (bf16[1536,128]{1,0:T(8,128)(2,1)S(1)}, bf16[1536,128]{1,0:T(8,128)(2,1)S(1)}, u32[]{:S(2)}, u32[]{:S(2)}) collective-permute-start(bf16[1536,128]{1,0:T(8,128)(2,1)S(1)} %fusion.2.a0), channel_id=1, source_target_pairs={{0,8},{8,16},{16,24},{24,0},{1,9},{9,17},{17,25},{25,1},{2,10},{10... | collective-permute-start | bytes 1179656 | tf_op jit(solution)/shard_map/ppermute | solution.py:313
  64.6 5.3 %collective-permute-start.3 = (bf16[2,32,1152]{2,1,0:T(8,128)(2,1)S(1)}, bf16[2,32,1152]{2,1,0:T(8,128)(2,1)S(1)}, u32[]{:S(2)}, u32[]{:S(2)}) collective-permute-start(bf16[2,32,1152]{2,1,0:T(8,128)(2,1)S(1)} %copy-done.21), channel_id=1, source_target_pairs={{0,1},{1,0},{8,9},{9,8},{16,17},{17,16},{24,25},{25,24},{2,3},{3,2... | collective-permute-start | bytes 442376 | tf_op jit(solution)/shard_map/ppermute | solution.py:322
  66.5 16.7 %collective-permute-start.4 = (bf16[2,32,1152]{2,1,0:T(8,128)(2,1)S(1)}, bf16[2,32,1152]{2,1,0:T(8,128)(2,1)S(1)}, u32[]{:S(2)}, u32[]{:S(2)}) collective-permute-start(bf16[2,32,1152]{2,1,0:T(8,128)(2,1)S(1)} %copy-done.20), channel_id=1, source_target_pairs={{0,8},{1,9},{8,16},{9,17},{16,24},{17,25},{24,0},{25,1},{2,10},{3,... | collective-permute-start | bytes 442376 | tf_op jit(solution)/shard_map/ppermute | solution.py:322
  69.9 23.8 %copy-start.18 = (bf16[2,32,1152]{2,1,0:T(8,128)(2,1)}, bf16[2,32,1152]{2,1,0:T(8,128)(2,1)S(1)}, u32[]{:S(2)}) copy-start(bf16[2,32,1152]{2,1,0:T(8,128)(2,1)S(1)} %collective-permute-done.3.refs_1_) | copy-start | bytes 442372
  69.9 39.0 %collective-permute-start.5 = (bf16[2,32,1152]{2,1,0:T(8,128)(2,1)}, bf16[2,32,1152]{2,1,0:T(8,128)(2,1)}, u32[]{:S(2)}, u32[]{:S(2)}) collective-permute-start(bf16[2,32,1152]{2,1,0:T(8,128)(2,1)} %get-tuple-element.103), channel_id=1, source_target_pairs={{0,9},{1,8},{8,17},{9,16},{16,25},{17,24},{24,1},{25,0},{2,11},{3,... | collective-permute-start | bytes 442376 | tf_op jit(solution)/shard_map/ppermute | solution.py:322
  83.2 10.6 %copy-start.19 = (bf16[2,32,1152]{2,1,0:T(8,128)(2,1)}, bf16[2,32,1152]{2,1,0:T(8,128)(2,1)S(1)}, u32[]{:S(2)}) copy-start(bf16[2,32,1152]{2,1,0:T(8,128)(2,1)S(1)} %collective-permute-done.4.refs_2_) | copy-start | bytes 442372
  83.2 25.7 %collective-permute-start.6 = (bf16[2,32,1152]{2,1,0:T(8,128)(2,1)}, bf16[2,32,1152]{2,1,0:T(8,128)(2,1)}, u32[]{:S(2)}, u32[]{:S(2)}) collective-permute-start(bf16[2,32,1152]{2,1,0:T(8,128)(2,1)} %get-tuple-element.104), channel_id=1, source_target_pairs={{0,16},{1,17},{8,24},{9,25},{16,0},{17,1},{24,8},{25,9},{2,18},{3,... | collective-permute-start | bytes 442376 | tf_op jit(solution)/shard_map/ppermute | solution.py:322
  87.3 21.6 %collective-permute-start.7 = (bf16[2,32,1152]{2,1,0:T(8,128)(2,1)}, bf16[2,32,1152]{2,1,0:T(8,128)(2,1)}, u32[]{:S(2)}, u32[]{:S(2)}) collective-permute-start(bf16[2,32,1152]{2,1,0:T(8,128)(2,1)} %get-tuple-element.105), channel_id=1, source_target_pairs={{0,17},{1,16},{8,25},{9,24},{16,1},{17,0},{24,9},{25,8},{2,19},{3,... | collective-permute-start | bytes 442376 | tf_op jit(solution)/shard_map/ppermute | solution.py:322
  90.0 18.9 %collective-permute-start.8 = (bf16[2,32,1152]{2,1,0:T(8,128)(2,1)}, bf16[2,32,1152]{2,1,0:T(8,128)(2,1)}, u32[]{:S(2)}, u32[]{:S(2)}) collective-permute-start(bf16[2,32,1152]{2,1,0:T(8,128)(2,1)} %get-tuple-element.106), channel_id=1, source_target_pairs={{0,24},{1,25},{8,0},{9,1},{16,8},{17,9},{24,16},{25,17},{2,26},{3,... | collective-permute-start | bytes 442376 | tf_op jit(solution)/shard_map/ppermute | solution.py:322
  94.5 14.4 %collective-permute-start.9 = (bf16[2,32,1152]{2,1,0:T(8,128)(2,1)}, bf16[2,32,1152]{2,1,0:T(8,128)(2,1)}, u32[]{:S(2)}, u32[]{:S(2)}) collective-permute-start(bf16[2,32,1152]{2,1,0:T(8,128)(2,1)} %get-tuple-element.107), channel_id=1, source_target_pairs={{0,25},{1,24},{8,1},{9,0},{16,9},{17,8},{24,17},{25,16},{2,27},{3,... | collective-permute-start | bytes 442376 | tf_op jit(solution)/shard_map/ppermute | solution.py:322
  112.8 130.5 %all-to-all-start.3 = ((bf16[4,2,40,1152]{3,2,1,0:T(8,128)(2,1)}), bf16[4,2,40,1152]{3,2,1,0:T(8,128)(2,1)}, u32[]{:S(2)}, u32[]{:S(2)}) async-start(bf16[4,2,40,1152]{3,2,1,0:T(8,128)(2,1)} %copy-done.1), calls=%async_computation.3 | async-start | bytes 1474560 | tf_op jit(solution)/shard_map/all_to_all | solution.py:308
  132.4 9.8 %collective-permute-start.10 = (bf16[288,128]{1,0:T(8,128)(2,1)S(1)}, bf16[288,128]{1,0:T(8,128)(2,1)S(1)}, u32[]{:S(2)}, u32[]{:S(2)}) collective-permute-start(bf16[288,128]{1,0:T(8,128)(2,1)S(1)} %get-tuple-element.114), channel_id=1, source_target_pairs={{0,8},{8,16},{16,24},{24,0},{1,9},{9,17},{17,25},{25,1},{2,10},{10... | collective-permute-start | bytes 221192 | tf_op jit(solution)/shard_map/ppermute | solution.py:313
  134.3 8.3 %collective-permute-start.11 = (bf16[288,128]{1,0:T(8,128)(2,1)S(1)}, bf16[288,128]{1,0:T(8,128)(2,1)S(1)}, u32[]{:S(2)}, u32[]{:S(2)}) collective-permute-start(bf16[288,128]{1,0:T(8,128)(2,1)S(1)} %get-tuple-element.115), channel_id=1, source_target_pairs={{0,16},{8,24},{16,0},{24,8},{1,17},{9,25},{17,1},{25,9},{2,18},{10... | collective-permute-start | bytes 221192 | tf_op jit(solution)/shard_map/ppermute | solution.py:313
  139.7 6.2 %collective-permute-start.12 = (bf16[288,128]{1,0:T(8,128)(2,1)S(1)}, bf16[288,128]{1,0:T(8,128)(2,1)S(1)}, u32[]{:S(2)}, u32[]{:S(2)}) collective-permute-start(bf16[288,128]{1,0:T(8,128)(2,1)S(1)} %get-tuple-element.116), channel_id=1, source_target_pairs={{0,24},{8,0},{16,8},{24,16},{1,25},{9,1},{17,9},{25,17},{2,26},{10... | collective-permute-start | bytes 221192 | tf_op jit(solution)/shard_map/ppermute | solution.py:313
  151.5 91.9 %copy-start.17 = (bf16[2,32,1152]{2,1,0:T(8,128)(2,1)S(1)}, bf16[2,32,1152]{2,1,0:T(8,128)(2,1)}, u32[]{:S(2)}) copy-start(bf16[2,32,1152]{2,1,0:T(8,128)(2,1)} %get-tuple-element.100.refs_0_) | copy-start | bytes 442372
  155.9 3.8 %collective-permute-start.13 = (bf16[4,4,128,128]{3,2,1,0:T(8,128)(2,1)S(1)}, bf16[4,4,128,128]{3,2,1,0:T(8,128)(2,1)S(1)}, u32[]{:S(2)}, u32[]{:S(2)}) collective-permute-start(bf16[4,4,128,128]{3,2,1,0:T(8,128)(2,1)S(1)} %get-tuple-element.118), channel_id=1, source_target_pairs={{0,1},{1,0},{2,3},{3,2},{4,5},{5,4},{6,7},{7,6},{8,9},{9,8},{10,11... | collective-permute-start | bytes 1572872 | tf_op jit(solution)/shard_map/ppermute | solution.py:313
  159.8 8.6 %collective-permute-start.14 = (bf16[4,128,128]{2,1,0:T(8,128)(2,1)S(1)}, bf16[4,128,128]{2,1,0:T(8,128)(2,1)S(1)}, u32[]{:S(2)}, u32[]{:S(2)}) collective-permute-start(bf16[4,128,128]{2,1,0:T(8,128)(2,1)S(1)} %get-tuple-element.120), channel_id=1, source_target_pairs={{0,32},{32,64},{64,96},{96,0},{1,33},{33,65},{65,97},{97,1},{2,34}... | collective-permute-start | bytes 393224 | tf_op jit(solution)/shard_map/ppermute | solution.py:313
  162.0 8.7 %collective-permute-start.15 = (bf16[4,128,128]{2,1,0:T(8,128)(2,1)S(1)}, bf16[4,128,128]{2,1,0:T(8,128)(2,1)S(1)}, u32[]{:S(2)}, u32[]{:S(2)}) collective-permute-start(bf16[4,128,128]{2,1,0:T(8,128)(2,1)S(1)} %get-tuple-element.121), channel_id=1, source_target_pairs={{0,64},{32,96},{64,0},{96,32},{1,65},{33,97},{65,1},{97,33},{2,66}... | collective-permute-start | bytes 393224 | tf_op jit(solution)/shard_map/ppermute | solution.py:313
  166.5 8.1 %collective-permute-start.16 = (bf16[4,128,128]{2,1,0:T(8,128)(2,1)S(1)}, bf16[4,128,128]{2,1,0:T(8,128)(2,1)S(1)}, u32[]{:S(2)}, u32[]{:S(2)}) collective-permute-start(bf16[4,128,128]{2,1,0:T(8,128)(2,1)S(1)} %get-tuple-element.122), channel_id=1, source_target_pairs={{0,96},{32,0},{64,32},{96,64},{1,97},{33,1},{65,33},{97,65},{2,98}... | collective-permute-start | bytes 393224 | tf_op jit(solution)/shard_map/ppermute | solution.py:313
  175.2 40.6 %collective-permute-start.17 = (bf16[2,128,128]{2,1,0:T(8,128)(2,1)S(1)}, bf16[2,128,128]{2,1,0:T(8,128)(2,1)S(1)}, u32[]{:S(2)}, u32[]{:S(2)}) collective-permute-start(bf16[2,128,128]{2,1,0:T(8,128)(2,1)S(1)} %get-tuple-element.124), channel_id=1, source_target_pairs={{0,4},{2,6},{4,0},{6,2},{1,5},{3,7},{5,1},{7,3},{8,12},{10,14},{12... | collective-permute-start | bytes 196616 | tf_op jit(solution)/shard_map/ppermute | solution.py:317
  215.8 26.9 %collective-permute-start.18 = (f32[128,128]{1,0:T(8,128)S(1)}, f32[128,128]{1,0:T(8,128)S(1)}, u32[]{:S(2)}, u32[]{:S(2)}) collective-permute-start(f32[128,128]{1,0:T(8,128)S(1)} %get-tuple-element.126), channel_id=1, source_target_pairs={{0,2},{2,0},{4,6},{6,4},{1,3},{3,1},{5,7},{7,5},{8,10},{10,8},{12,... | collective-permute-start | bytes 196616 | tf_op jit(solution)/shard_map/ppermute | solution.py:317
  243.4 13.9 %all-to-all-start.4 = ((bf16[8,16,128]{2,1,0:T(8,128)(2,1)}), bf16[8,16,128]{2,1,0:T(8,128)(2,1)S(1)}, u32[]{:S(2)}, u32[]{:S(2)}) async-start(bf16[8,16,128]{2,1,0:T(8,128)(2,1)} %shard_map.131), calls=%async_computation.4 | async-start | bytes 65536 | tf_op jit(solution)/shard_map/all_to_all | solution.py:308
  (15 other events, 18.7 us)
